TPU v7x, 32 devices: a whole 2x2x4 slice. The times are simulated.
32 devices in a mesh: segment: 4 (over y, x), frame: 2 (over core), row: 4 (over z).
Axes of the slice: x: 2, y: 2, z: 4, core: 2. Of those that a mesh axis runs over, the one named last changes fastest.
Arguments:
- latents: bfloat16 [2, 4, 8, 24, 320], P(None, 'frame', 'row')
- cotangent: bfloat16 [2, 4, 8, 24, 320], P(None, 'frame', 'row'), may hold values from -0.15625 to 0.15625
- timesteps: int32 [2], replicated, may hold values from 0 to 999
- frame_counts: int32 [2], replicated, may hold values from 1 to 4, as said below
- spatial_weight: bfloat16 [4, 9, 320, 320], P('segment'), may hold values from -0.109375 to 0.109375
- temporal_weight: bfloat16 [4, 3, 320, 320], P('segment'), may hold values from -0.1875 to 0.1875
- time_weight: bfloat16 [4, 1280, 320], P('segment'), may hold values from -0.15625 to 0.15625
- norm_gain: float32 [4, 320], P('segment'), may hold values from 0.5 to 1.5
Outputs:
- spatial_grad: float32 [4, 2880, 320], P('segment', ('frame', 'row'))
- temporal_grad: float32 [4, 960, 320], P('segment', ('frame', 'row'))
- time_grad: float32 [4, 1280, 320], P('segment', ('frame', 'row'))
- gain_grad: float32 [4, 320], P('segment', ('frame', 'row'))
Inputs may be any that keep to these rules, and one draw needn't show every extreme that they name: Frames frame_counts[c] and later of clip c are padding; some clip has all 4 frames.
All inputs are finite; a program needn't handle non-finite values.
Results may differ from a plain program's by a relative error of at most 0.02.
Values may be sent and summed in bfloat16 or wider, within the bound.
A program may use at most 128 MiB of HBM per device.

v0:
```python
import jax
import jax.numpy as jnp
from jax import lax
from jax.sharding import PartitionSpec as P

C = 320
G = 32
TE = 1280
WIDTH = 24
R_DEV = 2
F_DEV = 2
CLIPS = 2


EPSILON = 1e-05


def with_halo(array, sides, width):
    for axis, dim in sides:
        peers, length = (lax.axis_size(axis), array.shape[dim])
        up = [(i, (i + 1) % peers) for i in range(peers - 1)]
        down = [(j, i) for i, j in up]
        last = lax.slice_in_dim(array, length - width, length, axis=dim)
        leading = lax.slice_in_dim(array, 0, width, axis=dim)
        before = lax.ppermute(last, axis, up)
        after = lax.ppermute(leading, axis, down)
        array = jnp.concatenate([before, array, after], axis=dim)
    return array


def shifted(array, axis, by):
    peers = lax.axis_size(axis)
    pairs = [(i, i + by) for i in range(peers) if 0 <= i + by < peers]
    return lax.ppermute(array, axis, pairs)


def time_features(timesteps):
    half_dim = TE // 2
    frequency = jnp.exp(-jnp.log(10000.0) * jnp.arange(half_dim).astype(jnp.float32) / half_dim)
    angles = timesteps.astype(jnp.float32)[:, None] * frequency[None, :]
    wave_parts = jnp.concatenate([jnp.cos(angles), jnp.sin(angles)], axis=1)
    return jax.nn.silu(wave_parts).astype(jnp.bfloat16)


def group_sum(values):
    per_channel = jnp.sum(values, axis=(0, 1, 2))
    return per_channel.reshape(G, -1).sum(axis=1)


def spread(values):
    return jnp.repeat(values, C // G)


def spatial_columns(padded, row_count, col_count):
    return jnp.concatenate(
        [
            padded[:, vertical : vertical + row_count, lateral : lateral + col_count, :]
            for vertical in range(3)
            for lateral in range(3)
        ],
        axis=-1,
    )


def flip_columns(padded, row_count, col_count):
    return jnp.concatenate(
        [
            padded[
                :, 2 - vertical : 2 - vertical + row_count, 2 - lateral : 2 - lateral + col_count, :
            ]
            for vertical in range(3)
            for lateral in range(3)
        ],
        axis=-1,
    )


def time_columns(padded, frame_count):
    return jnp.concatenate([padded[offset : offset + frame_count] for offset in range(3)], axis=-1)


def time_flip(padded, frame_count):
    return jnp.concatenate(
        [padded[2 - offset : 2 - offset + frame_count] for offset in range(3)], axis=-1
    )


def flat_dot(columns, matrix):
    return jnp.dot(columns.reshape(-1, matrix.shape[0]), matrix, preferred_element_type=jnp.float32)


def outer_dot(columns, right_side):
    return lax.dot_general(
        columns.reshape(-1, columns.shape[-1]),
        right_side.reshape(-1, right_side.shape[-1]),
        (((0,), (0,)), ((), ())),
        preferred_element_type=jnp.float32,
    )


def remember(store, value, clip_index, is_live):
    old_value = lax.dynamic_index_in_dim(store, clip_index, 0, keepdims=False)
    return lax.dynamic_update_index_in_dim(
        store, jnp.where(is_live, value, old_value), clip_index, 0
    )


def pick_row(table, clip_index):
    return lax.dynamic_index_in_dim(table, clip_index, 0, keepdims=False)


def per_device(
    latents,
    cotangent,
    timesteps,
    frame_counts,
    spatial_weight,
    temporal_weight,
    time_weight,
    norm_gain,
):
    sections = lax.axis_size("segment")
    segment_index = lax.axis_index("segment")
    all_rows = R_DEV * lax.axis_size("row")
    group_width = C // G
    tick_total = CLIPS + sections - 1
    act_shape = (F_DEV, R_DEV, WIDTH, C)
    kernel = spatial_weight[0]
    tkernel = temporal_weight[0]
    gain_row = norm_gain[0]
    kernel_flat = kernel.reshape(9 * C, C)
    kernel_back = jnp.transpose(kernel, (0, 2, 1)).reshape(9 * C, C)
    tkernel_flat = tkernel.reshape(3 * C, C)
    tkernel_back = jnp.transpose(tkernel, (0, 2, 1)).reshape(3 * C, C)
    time_embed = time_features(timesteps)
    clip_biases = jnp.dot(time_embed, time_weight[0], preferred_element_type=jnp.float32)
    frame_ids = lax.axis_index("frame") * F_DEV + jnp.arange(F_DEV)
    zero_act = jnp.zeros(act_shape, jnp.bfloat16)

    def frame_mask_of(clip_index):
        frame_limit = pick_row(frame_counts, clip_index)
        frame_mask = (frame_ids < frame_limit).astype(jnp.float32)[:, None, None, None]
        cell_total = frame_limit.astype(jnp.float32) * all_rows * WIDTH * group_width
        return (frame_mask, cell_total)

    padded_in_store = jnp.zeros((CLIPS, F_DEV, R_DEV + 2, WIDTH + 2, C), jnp.bfloat16)
    hidden_store = jnp.zeros((CLIPS,) + act_shape, jnp.float32)
    padded_act_store = jnp.zeros((CLIPS, F_DEV + 2, R_DEV, WIDTH, C), jnp.bfloat16)
    mean_store = jnp.zeros((CLIPS, G), jnp.float32)
    inverse_store = jnp.zeros((CLIPS, G), jnp.float32)
    received = zero_act
    skip_queue = []
    for tick_step in range(tick_total):
        clip_raw = tick_step - segment_index
        is_live = (clip_raw >= 0) & (clip_raw < CLIPS)
        clip_index = jnp.clip(clip_raw, 0, CLIPS - 1)
        first_input = latents[min(tick_step, CLIPS - 1)]
        current = jnp.where(segment_index == 0, first_input, received)
        arriving = skip_queue[tick_step - sections + 1] if tick_step >= sections - 1 else zero_act
        joined = (current.astype(jnp.float32) + arriving.astype(jnp.float32)).astype(jnp.bfloat16)
        current = jnp.where(segment_index == sections - 1, joined, current)
        frame_mask, cell_total = frame_mask_of(clip_index)
        padded_rows = with_halo(current, (("row", 1),), 1)
        padded_in = jnp.pad(padded_rows, ((0, 0), (0, 0), (1, 1), (0, 0)))
        hidden = flat_dot(spatial_columns(padded_in, R_DEV, WIDTH), kernel_flat).reshape(
            act_shape
        ) + pick_row(clip_biases, clip_index)
        masked = hidden * frame_mask
        first_sums, square_sums = lax.psum(
            (group_sum(masked), group_sum(masked * hidden)), ("frame", "row")
        )
        group_mean = first_sums / cell_total
        variance = square_sums / cell_total - group_mean * group_mean
        centred = hidden - spread(group_mean)
        inv_spread = lax.rsqrt(variance + EPSILON)
        normed = centred * spread(inv_spread)
        activated = (frame_mask * jax.nn.silu(normed * gain_row)).astype(jnp.bfloat16)
        padded_act = with_halo(activated, (("frame", 0),), 1)
        temporal = flat_dot(time_columns(padded_act, F_DEV), tkernel_flat).reshape(act_shape)
        output = (current.astype(jnp.float32) + temporal).astype(jnp.bfloat16)
        padded_in_store = remember(padded_in_store, padded_in, clip_index, is_live)
        hidden_store = remember(hidden_store, hidden, clip_index, is_live)
        padded_act_store = remember(padded_act_store, padded_act, clip_index, is_live)
        mean_store = remember(mean_store, group_mean, clip_index, is_live)
        inverse_store = remember(inverse_store, inv_spread, clip_index, is_live)
        received = shifted(output, "segment", 1)
        skip_queue.append(shifted(output, "segment", sections - 1))
    spatial_acc = jnp.zeros((9 * C, C), jnp.float32)
    temporal_acc = jnp.zeros((3 * C, C), jnp.float32)
    gain_acc = jnp.zeros((C,), jnp.float32)
    time_acc = jnp.zeros((TE, C), jnp.float32)
    upstream_recv = zero_act
    grad_queue = []
    for tick_step in range(tick_total):
        clip_raw = tick_step - (sections - 1 - segment_index)
        is_live = (clip_raw >= 0) & (clip_raw < CLIPS)
        clip_index = jnp.clip(clip_raw, 0, CLIPS - 1)
        frame_mask, cell_total = frame_mask_of(clip_index)
        last_grad = (frame_mask * pick_row(cotangent, clip_index).astype(jnp.float32)).astype(
            jnp.bfloat16
        )
        upstream = jnp.where(segment_index == sections - 1, last_grad, upstream_recv)
        arriving = grad_queue[tick_step - sections + 1] if tick_step >= sections - 1 else zero_act
        joined = (upstream.astype(jnp.float32) + arriving.astype(jnp.float32)).astype(jnp.bfloat16)
        upstream = jnp.where(segment_index == 0, joined, upstream)
        padded_in = pick_row(padded_in_store, clip_index)
        hidden = pick_row(hidden_store, clip_index)
        padded_act = pick_row(padded_act_store, clip_index)
        group_mean = pick_row(mean_store, clip_index)
        inv_spread = pick_row(inverse_store, clip_index)
        padded_up = with_halo(upstream, (("frame", 0),), 1)
        act_grad = flat_dot(time_flip(padded_up, F_DEV), tkernel_back).reshape(act_shape)
        temporal_part = outer_dot(time_columns(padded_act, F_DEV), upstream)
        normed = (hidden - spread(group_mean)) * spread(inv_spread)
        scaled = normed * gain_row
        gate_sig = jax.nn.sigmoid(scaled)
        scaled_grad = act_grad * frame_mask * gate_sig * (1.0 + scaled * (1.0 - gate_sig))
        gain_part = jnp.sum(scaled_grad * normed, axis=(0, 1, 2))
        normed_grad = scaled_grad * gain_row
        first_total, second_total = lax.psum(
            (group_sum(normed_grad), group_sum(normed_grad * normed)), ("frame", "row")
        )
        first_moment = first_total / cell_total
        second_moment = second_total / cell_total
        hidden_grad = (
            spread(inv_spread)
            * (normed_grad - frame_mask * (spread(first_moment) + normed * spread(second_moment)))
        ).astype(jnp.bfloat16)
        column_sums = jnp.sum(hidden_grad.astype(jnp.float32), axis=(0, 1, 2))
        spatial_part = outer_dot(spatial_columns(padded_in, R_DEV, WIDTH), hidden_grad)
        padded_grad = with_halo(hidden_grad, (("row", 1),), 1)
        padded_grad = jnp.pad(padded_grad, ((0, 0), (0, 0), (1, 1), (0, 0)))
        conv_back = flat_dot(flip_columns(padded_grad, R_DEV, WIDTH), kernel_back).reshape(
            act_shape
        )
        input_grad = (upstream.astype(jnp.float32) + conv_back).astype(jnp.bfloat16)
        spatial_acc = spatial_acc + jnp.where(is_live, spatial_part, 0.0)
        temporal_acc = temporal_acc + jnp.where(is_live, temporal_part, 0.0)
        gain_acc = gain_acc + jnp.where(is_live, gain_part, 0.0)
        embed_row = pick_row(time_embed, clip_index).astype(jnp.float32)
        time_acc = time_acc + jnp.where(is_live, embed_row[:, None] * column_sums[None, :], 0.0)
        upstream_recv = shifted(input_grad, "segment", -1)
        grad_queue.append(shifted(input_grad, "segment", -(sections - 1)))
    spatial_out, temporal_out, time_out, gain_out = (
        lax.psum_scatter(spatial_acc, ("frame", "row"), scatter_dimension=0, tiled=True),
        lax.psum_scatter(temporal_acc, ("frame", "row"), scatter_dimension=0, tiled=True),
        lax.psum_scatter(time_acc, ("frame", "row"), scatter_dimension=0, tiled=True),
        lax.psum_scatter(gain_acc, ("frame", "row"), scatter_dimension=0, tiled=True),
    )
    return (spatial_out[None], temporal_out[None], time_out[None], gain_out[None])


def solution(mesh):
    return jax.shard_map(
        per_device,
        mesh=mesh,
        in_specs=(
            P(None, "frame", "row", None, None),
            P(None, "frame", "row", None, None),
            P(),
            P(),
            P("segment", None, None, None),
            P("segment", None, None, None),
            P("segment", None, None),
            P("segment", None),
        ),
        out_specs=(
            P("segment", ("frame", "row"), None),
            P("segment", ("frame", "row"), None),
            P("segment", ("frame", "row"), None),
            P("segment", ("frame", "row")),
        ),
        check_vma=False,
    )
```

profile of v0, /device:TPU:0, one launch (start us, length us, event | category | flops | bytes accessed | tf_op | source)
XLA Modules:
  0.0 679.5 jit_solution(7820467181774278046)
XLA Ops:
  9.6 5.6 collective-permute-start
  41.0 2.3 copy.50
  43.3 2.5 copy.52
  49.5 16.8 %all-reduce.21 = (f32[32]{0:T(128)S(1)}, f32[32]{0:T(128)S(1)}) all-reduce(f32[32]{0:T(128)S(1)} %reduce_sum.451, f32[32]{0:T(128)S(1)} %reduce_sum.453), channel_id=1, replica_groups=mesh['segment'=4,'frame'=2,'row'=4] {'frame','row'}, use_global_device_ids=true, to_apply=%region_2.3 | all-reduce | flops 64 | bytes 512 | tf_op jit(solution)/shard_map/psum | solution.py:169
  69.5 3.6 collective-permute-start.2
  76.2 3.5 collective-permute-start.4
  80.4 2.9 collective-permute-start.15
  84.6 4.5 collective-permute-start.5
  100.1 16.1 %all-reduce.20 = (f32[32]{0:T(128)S(1)}, f32[32]{0:T(128)S(1)}) all-reduce(f32[32]{0:T(128)} %reduce_sum.455, f32[32]{0:T(128)S(1)} %reduce_sum.457), channel_id=1, replica_groups=mesh['segment'=4,'frame'=2,'row'=4] {'frame','row'}, use_global_device_ids=true, to_apply=%region_8.9 | all-reduce | flops 64 | bytes 512 | tf_op jit(solution)/shard_map/psum | solution.py:169
  123.7 4.2 collective-permute-start.7
  133.6 3.0 collective-permute-start.9
  140.0 4.5 collective-permute-start.10
  149.6 2.3 fusion.126
  155.5 16.1 %all-reduce.19 = (f32[32]{0:T(128)S(1)}, f32[32]{0:T(128)S(1)}) all-reduce(f32[32]{0:T(128)} %reduce_sum.459, f32[32]{0:T(128)S(1)} %reduce_sum.461), channel_id=1, replica_groups=mesh['segment'=4,'frame'=2,'row'=4] {'frame','row'}, use_global_device_ids=true, to_apply=%region_14.15 | all-reduce | flops 64 | bytes 512 | tf_op jit(solution)/shard_map/psum | solution.py:169
  177.0 3.0 collective-permute-start.12
  183.5 5.9 collective-permute-start.21
  196.3 4.5 collective-permute-start.16
  206.0 2.3 fusion.127
  210.2 16.0 %all-reduce.18 = (f32[32]{0:T(128)S(1)}, f32[32]{0:T(128)S(1)}) all-reduce(f32[32]{0:T(128)S(1)} %reduce_sum.463, f32[32]{0:T(128)S(1)} %reduce_sum.465), channel_id=1, replica_groups=mesh['segment'=4,'frame'=2,'row'=4] {'frame','row'}, use_global_device_ids=true, to_apply=%region_20.21 | all-reduce | flops 64 | bytes 512 | tf_op jit(solution)/shard_map/psum | solution.py:169
  230.2 3.0 collective-permute-start.18
  235.6 4.3 collective-permute-start.20
  244.1 5.2 collective-permute-start.22
  257.9 15.1 %all-reduce.17 = (f32[32]{0:T(128)S(1)}, f32[32]{0:T(128)S(1)}) all-reduce(f32[32]{0:T(128)S(1)} %reduce_sum.469, f32[32]{0:T(128)S(1)} %reduce_sum.467), channel_id=1, replica_groups=mesh['segment'=4,'frame'=2,'row'=4] {'frame','row'}, use_global_device_ids=true, to_apply=%region_29.30 | all-reduce | flops 64 | bytes 512 | tf_op jit(solution)/shard_map/psum | solution.py:169
  274.7 2.7 multiply_reduce_fusion.9
  277.8 14.7 %all-reduce.16 = (f32[32]{0:T(128)S(1)}, f32[32]{0:T(128)S(1)}) all-reduce(f32[32]{0:T(128)S(1)} %reduce_sum.473, f32[32]{0:T(128)S(1)} %reduce_sum.471), channel_id=1, replica_groups=mesh['segment'=4,'frame'=2,'row'=4] {'frame','row'}, use_global_device_ids=true, to_apply=%region_35.36 | all-reduce | flops 64 | bytes 512 | tf_op jit(solution)/shard_map/psum | solution.py:220
  295.2 4.5 collective-permute-start.26
  308.7 4.8 collective-permute-done.28
  318.7 2.7 multiply_reduce_fusion.8
  321.9 17.5 %all-reduce.15 = (f32[32]{0:T(128)S(1)}, f32[32]{0:T(128)S(1)}) all-reduce(f32[32]{0:T(128)S(1)} %reduce_sum.477, f32[32]{0:T(128)S(1)} %reduce_sum.475), channel_id=1, replica_groups=mesh['segment'=4,'frame'=2,'row'=4] {'frame','row'}, use_global_device_ids=true, to_apply=%region_41.42 | all-reduce | flops 64 | bytes 512 | tf_op jit(solution)/shard_map/psum | solution.py:220
  342.2 4.5 collective-permute-start.31
  351.9 2.3 add_convert_fusion.4
  356.4 5.6 collective-permute-done.33
  367.9 2.8 multiply_reduce_fusion.7
  371.1 16.7 %all-reduce.14 = (f32[32]{0:T(128)S(1)}, f32[32]{0:T(128)S(1)}) all-reduce(f32[32]{0:T(128)S(1)} %reduce_sum.481, f32[32]{0:T(128)S(1)} %reduce_sum.479), channel_id=1, replica_groups=mesh['segment'=4,'frame'=2,'row'=4] {'frame','row'}, use_global_device_ids=true, to_apply=%region_47.48 | all-reduce | flops 64 | bytes 512 | tf_op jit(solution)/shard_map/psum | solution.py:220
  390.5 4.5 collective-permute-start.36
  405.2 4.6 collective-permute-done.38
  429.6 16.5 %all-reduce.13 = (f32[32]{0:T(128)S(1)}, f32[32]{0:T(128)S(1)}) all-reduce(f32[32]{0:T(128)S(1)} %reduce_sum.485, f32[32]{0:T(128)S(1)} %reduce_sum.483), channel_id=1, replica_groups=mesh['segment'=4,'frame'=2,'row'=4] {'frame','row'}, use_global_device_ids=true, to_apply=%region_53.54 | all-reduce | flops 64 | bytes 512 | tf_op jit(solution)/shard_map/psum | solution.py:220
  448.4 4.8 collective-permute-start.42
  453.2 3.6 fusion.5
  464.1 2.5 fusion.6
  466.7 3.2 collective-permute-done.44
  473.7 2.7 fusion.7
  477.3 13.7 %all-reduce.12 = (f32[32]{0:T(128)S(1)}, f32[32]{0:T(128)S(1)}, f32[320]{0:T(512)S(1)}) all-reduce(f32[32]{0:T(128)S(1)} %reduce_sum.489, f32[32]{0:T(128)S(1)} %reduce_sum.487, f32[320]{0:T(512)S(1)} %select_add_fusion.1), channel_id=1, replica_groups=mesh['segment'=4,'frame'=2,'row'=4] {'frame','row'}, use_global_device_ids=true, to_apply=%region_59.60 | all-reduce | flops 384 | bytes 3072 | tf_op jit(solution)/shard_map/psum | solution.py:220
  493.2 3.2 collective-permute-start.48
  497.1 6.5 fusion.4
  508.1 2.5 select_add_fusion
  513.7 109.3 %all-reduce.25.cloned.1.call-done = (f32[2880,320]{0,1:T(8,128)}, f32[960,320]{0,1:T(8,128)}) async-done(((f32[2880,320]{0,1:T(8,128)}, f32[960,320]{0,1:T(8,128)}), (f32[2880,320]{0,1:T(8,128)}, f32[960,320]{0,1:T(8,128)})) %all-reduce.25.cloned.1.call-update) | async-done | bytes 4915216
  626.8 45.8 %reduce-scatter.4.cloned.1.call-done = f32[160,320]{1,0:T(8,128)} async-done(((f32[1280,320]{1,0:T(8,128)}), f32[160,320]{1,0:T(8,128)}) %reduce-scatter.4.cloned.1.call-update) | async-done | bytes 204816 | tf_op jit(solution)/shard_map/reduce_scatter | solution.py:247
  (588 shorter events, 205.0 us)
Async XLA Ops:
  7.2 615.8 %all-reduce.25.cloned.1.call-start = ((), (), s32[]{:S(2)}) async-start(), calls=%async_computation.2 | async-start | bytes 10158080
  8.3 38.2 %collective-permute-start.1 = (bf16[2,1,24,320]{3,2,1,0:T(8,128)(2,1)S(1)}, bf16[2,1,24,320]{3,2,1,0:T(8,128)(2,1)S(1)}, u32[]{:S(2)}, u32[]{:S(2)}) collective-permute-start(bf16[2,1,24,320]{3,2,1,0:T(8,128)(2,1)S(1)} %get-tuple-element.266), channel_id=1, source_target_pairs={{1,0},{2,1},{3,2},{5,4},{6,5},{7,6},{9,8},{10,9},{11,10},{13,12},{... | collective-permute-start | bytes 92168 | tf_op jit(solution)/shard_map/ppermute | solution.py:26
  9.6 36.9 %collective-permute-start = (bf16[2,1,24,320]{3,2,1,0:T(8,128)(2,1)S(1)}, bf16[2,1,24,320]{3,2,1,0:T(8,128)(2,1)S(1)}, u32[]{:S(2)}, u32[]{:S(2)}) collective-permute-start(bf16[2,1,24,320]{3,2,1,0:T(8,128)(2,1)S(1)} %get-tuple-element.265), channel_id=1, source_target_pairs={{0,1},{1,2},{2,3},{4,5},{5,6},{6,7},{8,9},{9,10},{10,11},{12,13},{... | collective-permute-start | bytes 92168 | tf_op jit(solution)/shard_map/ppermute | solution.py:25
  19.3 255.3 %collective-permute-start.25 = (bf16[1,2,24,320]{3,2,1,0:T(8,128)(2,1)}, bf16[1,2,24,320]{3,2,1,0:T(8,128)(2,1)}, u32[]{:S(2)}, u32[]{:S(2)}) collective-permute-start(bf16[1,2,24,320]{3,2,1,0:T(8,128)(2,1)} %get-tuple-element.240), channel_id=1, source_target_pairs={{0,4},{1,5},{2,6},{3,7},{8,12},{9,13},{10,14},{11,15},{16,20},{17,... | collective-permute-start | bytes 92168 | tf_op jit(solution)/shard_map/ppermute | solution.py:25
  21.3 253.3 %collective-permute-start.24 = (bf16[1,2,24,320]{3,2,1,0:T(8,128)(2,1)}, bf16[1,2,24,320]{3,2,1,0:T(8,128)(2,1)}, u32[]{:S(2)}, u32[]{:S(2)}) collective-permute-start(bf16[1,2,24,320]{3,2,1,0:T(8,128)(2,1)} %get-tuple-element.239), channel_id=1, source_target_pairs={{4,0},{5,1},{6,2},{7,3},{12,8},{13,9},{14,10},{15,11},{20,16},{21,... | collective-permute-start | bytes 92168 | tf_op jit(solution)/shard_map/ppermute | solution.py:26
  68.2 5.9 collective-permute-start.3
  69.5 4.7 collective-permute-start.2
  76.2 7.1 %collective-permute-start.4 = (bf16[2,2,24,320]{3,2,1,0:T(8,128)(2,1)}, bf16[2,2,24,320]{3,2,1,0:T(8,128)(2,1)S(1)}, u32[]{:S(2)}, u32[]{:S(2)}) collective-permute-start(bf16[2,2,24,320]{3,2,1,0:T(8,128)(2,1)} %fusion.28), channel_id=1, source_target_pairs={{0,8},{8,16},{16,24},{1,9},{9,17},{17,25},{2,10},{10,18},{18,26},{... | collective-permute-start | bytes 184328 | tf_op jit(solution)/shard_map/ppermute | solution.py:34
  80.4 112.4 %collective-permute-start.15 = (bf16[2,2,24,320]{3,2,1,0:T(8,128)(2,1)}, bf16[2,2,24,320]{3,2,1,0:T(8,128)(2,1)}, u32[]{:S(2)}, u32[]{:S(2)}) collective-permute-start(bf16[2,2,24,320]{3,2,1,0:T(8,128)(2,1)} %fusion.28), channel_id=1, source_target_pairs={{0,24},{1,25},{2,26},{3,27},{4,28},{5,29},{6,30},{7,31}} | collective-permute-start | bytes 184328 | tf_op jit(solution)/shard_map/ppermute | solution.py:34
  83.3 6.7 collective-permute-start.6
  84.6 6.2 collective-permute-start.5
  122.4 9.6 %collective-permute-start.8 = (bf16[1,2,24,320]{3,2,1,0:T(8,128)(2,1)}, bf16[1,2,24,320]{3,2,1,0:T(8,128)(2,1)}, u32[]{:S(2)}, u32[]{:S(2)}) collective-permute-start(bf16[1,2,24,320]{3,2,1,0:T(8,128)(2,1)} %get-tuple-element.256), channel_id=1, source_target_pairs={{4,0},{5,1},{6,2},{7,3},{12,8},{13,9},{14,10},{15,11},{20,16},{21,... | collective-permute-start | bytes 92168 | tf_op jit(solution)/shard_map/ppermute | solution.py:26
  123.7 8.4 %collective-permute-start.7 = (bf16[1,2,24,320]{3,2,1,0:T(8,128)(2,1)}, bf16[1,2,24,320]{3,2,1,0:T(8,128)(2,1)}, u32[]{:S(2)}, u32[]{:S(2)}) collective-permute-start(bf16[1,2,24,320]{3,2,1,0:T(8,128)(2,1)} %get-tuple-element.255), channel_id=1, source_target_pairs={{0,4},{1,5},{2,6},{3,7},{8,12},{9,13},{10,14},{11,15},{16,20},{17,... | collective-permute-start | bytes 92168 | tf_op jit(solution)/shard_map/ppermute | solution.py:25
  133.6 5.0 collective-permute-start.9
  138.7 6.7 collective-permute-start.11
  140.0 6.2 collective-permute-start.10
  175.7 7.7 %collective-permute-start.13 = (bf16[1,2,24,320]{3,2,1,0:T(8,128)(2,1)S(1)}, bf16[1,2,24,320]{3,2,1,0:T(8,128)(2,1)S(1)}, u32[]{:S(2)}, u32[]{:S(2)}) collective-permute-start(bf16[1,2,24,320]{3,2,1,0:T(8,128)(2,1)S(1)} %get-tuple-element.250), channel_id=1, source_target_pairs={{4,0},{5,1},{6,2},{7,3},{12,8},{13,9},{14,10},{15,11},{20,16},{21,... | collective-permute-start | bytes 92168 | tf_op jit(solution)/shard_map/ppermute | solution.py:26
  177.0 12.3 %collective-permute-start.12 = (bf16[1,2,24,320]{3,2,1,0:T(8,128)(2,1)S(1)}, bf16[1,2,24,320]{3,2,1,0:T(8,128)(2,1)S(1)}, u32[]{:S(2)}, u32[]{:S(2)}) collective-permute-start(bf16[1,2,24,320]{3,2,1,0:T(8,128)(2,1)S(1)} %get-tuple-element.249), channel_id=1, source_target_pairs={{0,4},{1,5},{2,6},{3,7},{8,12},{9,13},{10,14},{11,15},{16,20},{17,... | collective-permute-start | bytes 92168 | tf_op jit(solution)/shard_map/ppermute | solution.py:25
  183.5 56.5 %collective-permute-start.21 = (bf16[2,2,24,320]{3,2,1,0:T(8,128)(2,1)}, bf16[2,2,24,320]{3,2,1,0:T(8,128)(2,1)}, u32[]{:S(2)}, u32[]{:S(2)}) collective-permute-start(bf16[2,2,24,320]{3,2,1,0:T(8,128)(2,1)} %copy-done.107), channel_id=1, source_target_pairs={{0,24},{1,25},{2,26},{3,27},{4,28},{5,29},{6,30},{7,31}} | collective-permute-start | bytes 184328 | tf_op jit(solution)/shard_map/ppermute | solution.py:34
  195.0 6.6 collective-permute-start.17
  196.3 6.2 collective-permute-start.16
  228.9 5.2 collective-permute-start.19
  235.6 6.2 collective-permute-start.20
  242.8 7.9 %collective-permute-start.23 = (bf16[2,1,24,320]{3,2,1,0:T(8,128)(2,1)S(1)}, bf16[2,1,24,320]{3,2,1,0:T(8,128)(2,1)S(1)}, u32[]{:S(2)}, u32[]{:S(2)}) collective-permute-start(bf16[2,1,24,320]{3,2,1,0:T(8,128)(2,1)S(1)} %get-tuple-element.242), channel_id=1, source_target_pairs={{1,0},{2,1},{3,2},{5,4},{6,5},{7,6},{9,8},{10,9},{11,10},{13,12},{... | collective-permute-start | bytes 92168 | tf_op jit(solution)/shard_map/ppermute | solution.py:26
  244.1 7.2 %collective-permute-start.22 = (bf16[2,1,24,320]{3,2,1,0:T(8,128)(2,1)S(1)}, bf16[2,1,24,320]{3,2,1,0:T(8,128)(2,1)}, u32[]{:S(2)}, u32[]{:S(2)}) collective-permute-start(bf16[2,1,24,320]{3,2,1,0:T(8,128)(2,1)S(1)} %get-tuple-element.241), channel_id=1, source_target_pairs={{0,1},{1,2},{2,3},{4,5},{5,6},{6,7},{8,9},{9,10},{10,11},{12,13},{... | collective-permute-start | bytes 92168 | tf_op jit(solution)/shard_map/ppermute | solution.py:25
  293.9 6.9 %collective-permute-start.27 = (bf16[2,1,24,320]{3,2,1,0:T(8,128)(2,1)S(1)}, bf16[2,1,24,320]{3,2,1,0:T(8,128)(2,1)S(1)}, u32[]{:S(2)}, u32[]{:S(2)}) collective-permute-start(bf16[2,1,24,320]{3,2,1,0:T(8,128)(2,1)S(1)} %get-tuple-element.236), channel_id=1, source_target_pairs={{1,0},{2,1},{3,2},{5,4},{6,5},{7,6},{9,8},{10,9},{11,10},{13,12},{... | collective-permute-start | bytes 92168 | tf_op jit(solution)/shard_map/ppermute | solution.py:26
  295.2 6.2 collective-permute-start.26
  306.6 6.8 %collective-permute-start.28 = (bf16[2,2,24,320]{3,2,1,0:T(8,128)(2,1)S(1)}, bf16[2,2,24,320]{3,2,1,0:T(8,128)(2,1)S(1)}, u32[]{:S(2)}, u32[]{:S(2)}) collective-permute-start(bf16[2,2,24,320]{3,2,1,0:T(8,128)(2,1)S(1)} %fusion.29), channel_id=1, source_target_pairs={{8,0},{16,8},{24,16},{9,1},{17,9},{25,17},{10,2},{18,10},{26,18},{... | collective-permute-start | bytes 184328 | tf_op jit(solution)/shard_map/ppermute | solution.py:34
  313.6 4.9 collective-permute-start.30
  340.9 6.8 %collective-permute-start.32 = (bf16[2,1,24,320]{3,2,1,0:T(8,128)(2,1)S(1)}, bf16[2,1,24,320]{3,2,1,0:T(8,128)(2,1)S(1)}, u32[]{:S(2)}, u32[]{:S(2)}) collective-permute-start(bf16[2,1,24,320]{3,2,1,0:T(8,128)(2,1)S(1)} %get-tuple-element.230), channel_id=1, source_target_pairs={{1,0},{2,1},{3,2},{5,4},{6,5},{7,6},{9,8},{10,9},{11,10},{13,12},{... | collective-permute-start | bytes 92168 | tf_op jit(solution)/shard_map/ppermute | solution.py:26
  342.2 6.2 collective-permute-start.31
  354.2 7.8 %collective-permute-start.33 = (bf16[2,2,24,320]{3,2,1,0:T(8,128)(2,1)}, bf16[2,2,24,320]{3,2,1,0:T(8,128)(2,1)S(1)}, u32[]{:S(2)}, u32[]{:S(2)}) collective-permute-start(bf16[2,2,24,320]{3,2,1,0:T(8,128)(2,1)} %add_convert_fusion.4), channel_id=1, source_target_pairs={{8,0},{16,8},{24,16},{9,1},{17,9},{25,17},{10,2},{18,10},{26,18},{... | collective-permute-start | bytes 184328 | tf_op jit(solution)/shard_map/ppermute | solution.py:34
  362.8 4.5 collective-permute-start.35
  389.2 8.3 %collective-permute-start.37 = (bf16[2,1,24,320]{3,2,1,0:T(8,128)(2,1)S(1)}, bf16[2,1,24,320]{3,2,1,0:T(8,128)(2,1)S(1)}, u32[]{:S(2)}, u32[]{:S(2)}) collective-permute-start(bf16[2,1,24,320]{3,2,1,0:T(8,128)(2,1)S(1)} %get-tuple-element.224), channel_id=1, source_target_pairs={{1,0},{2,1},{3,2},{5,4},{6,5},{7,6},{9,8},{10,9},{11,10},{13,12},{... | collective-permute-start | bytes 92168 | tf_op jit(solution)/shard_map/ppermute | solution.py:26
  390.5 7.0 %collective-permute-start.36 = (bf16[2,1,24,320]{3,2,1,0:T(8,128)(2,1)S(1)}, bf16[2,1,24,320]{3,2,1,0:T(8,128)(2,1)S(1)}, u32[]{:S(2)}, u32[]{:S(2)}) collective-permute-start(bf16[2,1,24,320]{3,2,1,0:T(8,128)(2,1)S(1)} %get-tuple-element.223), channel_id=1, source_target_pairs={{0,1},{1,2},{2,3},{4,5},{5,6},{6,7},{8,9},{9,10},{10,11},{12,13},{... | collective-permute-start | bytes 92168 | tf_op jit(solution)/shard_map/ppermute | solution.py:25
  396.2 9.0 %collective-permute-start.39 = (bf16[2,2,24,320]{3,2,1,0:T(8,128)(2,1)}, bf16[2,2,24,320]{3,2,1,0:T(8,128)(2,1)}, u32[]{:S(2)}, u32[]{:S(2)}) collective-permute-start(bf16[2,2,24,320]{3,2,1,0:T(8,128)(2,1)} %copy-done.61), channel_id=1, source_target_pairs={{24,0},{25,1},{26,2},{27,3},{28,4},{29,5},{30,6},{31,7}} | collective-permute-start | bytes 184328 | tf_op jit(solution)/shard_map/ppermute | solution.py:34
  402.7 7.1 %collective-permute-start.38 = (bf16[2,2,24,320]{3,2,1,0:T(8,128)(2,1)S(1)}, bf16[2,2,24,320]{3,2,1,0:T(8,128)(2,1)S(1)}, u32[]{:S(2)}, u32[]{:S(2)}) collective-permute-start(bf16[2,2,24,320]{3,2,1,0:T(8,128)(2,1)S(1)} %add_convert_fusion.3), channel_id=1, source_target_pairs={{8,0},{16,8},{24,16},{9,1},{17,9},{25,17},{10,2},{18,10},{26,18},{... | collective-permute-start | bytes 184328 | tf_op jit(solution)/shard_map/ppermute | solution.py:34
  411.5 15.5 %collective-permute-start.41 = (bf16[1,2,24,320]{3,2,1,0:T(8,128)(2,1)}, bf16[1,2,24,320]{3,2,1,0:T(8,128)(2,1)}, u32[]{:S(2)}, u32[]{:S(2)}) collective-permute-start(bf16[1,2,24,320]{3,2,1,0:T(8,128)(2,1)} %get-tuple-element.220), channel_id=1, source_target_pairs={{0,4},{1,5},{2,6},{3,7},{8,12},{9,13},{10,14},{11,15},{16,20},{17,... | collective-permute-start | bytes 92168 | tf_op jit(solution)/shard_map/ppermute | solution.py:25
  413.4 13.6 %collective-permute-start.40 = (bf16[1,2,24,320]{3,2,1,0:T(8,128)(2,1)S(1)}, bf16[1,2,24,320]{3,2,1,0:T(8,128)(2,1)}, u32[]{:S(2)}, u32[]{:S(2)}) collective-permute-start(bf16[1,2,24,320]{3,2,1,0:T(8,128)(2,1)S(1)} %get-tuple-element.219), channel_id=1, source_target_pairs={{4,0},{5,1},{6,2},{7,3},{12,8},{13,9},{14,10},{15,11},{20,16},{21,... | collective-permute-start | bytes 92168 | tf_op jit(solution)/shard_map/ppermute | solution.py:26
  447.1 11.1 %collective-permute-start.43 = (bf16[2,1,24,320]{3,2,1,0:T(8,128)(2,1)S(1)}, bf16[2,1,24,320]{3,2,1,0:T(8,128)(2,1)S(1)}, u32[]{:S(2)}, u32[]{:S(2)}) collective-permute-start(bf16[2,1,24,320]{3,2,1,0:T(8,128)(2,1)S(1)} %get-tuple-element.218), channel_id=1, source_target_pairs={{1,0},{2,1},{3,2},{5,4},{6,5},{7,6},{9,8},{10,9},{11,10},{13,12},{... | collective-permute-start | bytes 92168 | tf_op jit(solution)/shard_map/ppermute | solution.py:26
  448.4 9.8 %collective-permute-start.42 = (bf16[2,1,24,320]{3,2,1,0:T(8,128)(2,1)S(1)}, bf16[2,1,24,320]{3,2,1,0:T(8,128)(2,1)S(1)}, u32[]{:S(2)}, u32[]{:S(2)}) collective-permute-start(bf16[2,1,24,320]{3,2,1,0:T(8,128)(2,1)S(1)} %get-tuple-element.217), channel_id=1, source_target_pairs={{0,1},{1,2},{2,3},{4,5},{5,6},{6,7},{8,9},{9,10},{10,11},{12,13},{... | collective-permute-start | bytes 92168 | tf_op jit(solution)/shard_map/ppermute | solution.py:25
  456.8 9.9 %collective-permute-start.45 = (bf16[2,2,24,320]{3,2,1,0:T(8,128)(2,1)}, bf16[2,2,24,320]{3,2,1,0:T(8,128)(2,1)}, u32[]{:S(2)}, u32[]{:S(2)}) collective-permute-start(bf16[2,2,24,320]{3,2,1,0:T(8,128)(2,1)} %add_convert_fusion.4), channel_id=1, source_target_pairs={{24,0},{25,1},{26,2},{27,3},{28,4},{29,5},{30,6},{31,7}} | collective-permute-start | bytes 184328 | tf_op jit(solution)/shard_map/ppermute | solution.py:34
  462.7 7.3 %collective-permute-start.44 = (bf16[2,2,24,320]{3,2,1,0:T(8,128)(2,1)S(1)}, bf16[2,2,24,320]{3,2,1,0:T(8,128)(2,1)S(1)}, u32[]{:S(2)}, u32[]{:S(2)}) collective-permute-start(bf16[2,2,24,320]{3,2,1,0:T(8,128)(2,1)S(1)} %add_convert_fusion.1), channel_id=1, source_target_pairs={{8,0},{16,8},{24,16},{9,1},{17,9},{25,17},{10,2},{18,10},{26,18},{... | collective-permute-start | bytes 184328 | tf_op jit(solution)/shard_map/ppermute | solution.py:34
  471.0 5.4 collective-permute-start.47
  472.4 4.0 collective-permute-start.46
  491.6 12.0 %collective-permute-start.49 = (bf16[1,2,24,320]{3,2,1,0:T(8,128)(2,1)S(1)}, bf16[1,2,24,320]{3,2,1,0:T(8,128)(2,1)S(1)}, u32[]{:S(2)}, u32[]{:S(2)}) collective-permute-start(bf16[1,2,24,320]{3,2,1,0:T(8,128)(2,1)S(1)} %get-tuple-element.212), channel_id=1, source_target_pairs={{4,0},{5,1},{6,2},{7,3},{12,8},{13,9},{14,10},{15,11},{20,16},{21,... | collective-permute-start | bytes 92168 | tf_op jit(solution)/shard_map/ppermute | solution.py:26
  493.2 10.5 %collective-permute-start.48 = (bf16[1,2,24,320]{3,2,1,0:T(8,128)(2,1)S(1)}, bf16[1,2,24,320]{3,2,1,0:T(8,128)(2,1)S(1)}, u32[]{:S(2)}, u32[]{:S(2)}) collective-permute-start(bf16[1,2,24,320]{3,2,1,0:T(8,128)(2,1)S(1)} %get-tuple-element.211), channel_id=1, source_target_pairs={{0,4},{1,5},{2,6},{3,7},{8,12},{9,13},{10,14},{11,15},{16,20},{17,... | collective-permute-start | bytes 92168 | tf_op jit(solution)/shard_map/ppermute | solution.py:25
  507.3 165.3 %reduce-scatter.4.cloned.1.call-start = ((), (), s32[]{:S(2)}) async-start(), calls=%async_computation.1 | async-start | bytes 2211840 | tf_op jit(solution)/shard_map/reduce_scatter | solution.py:247
  (113 other events, 1760.0 us)
Sparse Core Ops, SparseCore 0:
  507.4 115.5 all-reduce.24
  626.0 46.5 reduce-scatter.3
where the time goes:
time: 684 us; the launch traced here: 680 us
  waiting for transfers between devices  182 us (27%)
  blocking collectives  159 us (23%)
  starting transfers between devices  123 us (18%)
  local copies, waits for them, and re-layouts  81.5 us (12%)
  other arithmetic  55.8 us (8%)
  matrix products  53.3 us (8%)
  between operations  24.8 us (4%)
    unnamed x3, waiting for transfers between devices  109 us
    psum x5, blocking collectives, per_device(): lax.psum((group_sum(masked), group_sum(masked * hidden)), ('frame', 'row'))  80.2 us
    psum x5, blocking collectives, per_device(): lax.psum((group_sum(normed_grad), group_sum(normed_grad * normed)), ('fra...  79 us
    ppermute x19, starting transfers between devices, with_halo(): before = lax.ppermute(last, axis, up)  69 us
    reduce_scatter x1, waiting for transfers between devices, per_device(): lax.psum_scatter(time_acc, ('frame', 'row'), scatter_dimension=0, tiled=T...  45.8 us
    dot_general x18, matrix products, flat_dot(): jnp.dot(columns.reshape(-1, matrix.shape[0]), matrix, preferred_element_t...  33.7 us
    ppermute x12, starting transfers between devices, shifted(): return lax.ppermute(array, axis, pairs)  28.8 us
    ppermute x19, starting transfers between devices, with_halo(): after = lax.ppermute(leading, axis, down)  24.7 us
  transfers between devices with their start and end apart: 52, of which 16 were waited for; matrix products, arithmetic and copies ran while one was open for 22% of the time, Pallas kernels for 0%

commit v1 on v0

v1 whole, which is shorter than its diff:
```python
import functools

import jax
import jax.numpy as jnp
from jax import lax
from jax.experimental import pallas as pl
from jax.experimental.pallas import tpu as pltpu
from jax.sharding import PartitionSpec as P

C = 320
G = 32
TE = 1280
WIDTH = 24
R_DEV = 2
F_DEV = 2
CLIPS = 2


EPSILON = 1e-05


def time_features(timesteps):
    half_dim = TE // 2
    frequency = jnp.exp(-jnp.log(10000.0) * jnp.arange(half_dim).astype(jnp.float32) / half_dim)
    angles = timesteps.astype(jnp.float32)[:, None] * frequency[None, :]
    wave_parts = jnp.concatenate([jnp.cos(angles), jnp.sin(angles)], axis=1)
    return jax.nn.silu(wave_parts).astype(jnp.bfloat16)


PAD = 32
BLOCK = F_DEV * CLIPS * PAD
CELLS = R_DEV * BLOCK
HALF = CLIPS * PAD
MESH = pl.DeviceIdType.MESH


def swap_order(flat):
    return jnp.concatenate(
        [flat[:HALF], flat[2 * HALF : 3 * HALF], flat[HALF : 2 * HALF], flat[3 * HALF :]], axis=0
    )


def dot_nn(left, right):
    return lax.dot_general(left, right, (((1,), (0,)), ((), ())), preferred_element_type=jnp.float32)


def dot_nt(left, right):
    return lax.dot_general(left, right, (((1,), (1,)), ((), ())), preferred_element_type=jnp.float32)


def widen(padded, wide):
    values = padded[...]
    exact = values.astype(jnp.float32)
    length = values.shape[0]
    wide[0] = pltpu.roll(exact, 1, 0).astype(jnp.bfloat16)
    wide[1] = values
    wide[2] = pltpu.roll(exact, length - 1, 0).astype(jnp.bfloat16)


def section_kernel(
    sections, n_frame, n_row,
    first_x, last_up, bias, mask, width_mask, inv_total, kernel, tkernel, gain, groups,
    spatial_out, temporal_out, sums_out,
    x_in, skip_in, x_out, u_in, u_skip, u_out, pad_x, pad_a, pad_u, pad_h, wide_x, wide_h,
    x_turned, a_turned, normed, grads, stat_src, slots, send_sem, recv_sem,
):
    seg = lax.axis_index("segment")
    frame = lax.axis_index("frame")
    row = lax.axis_index("row")
    peers = n_frame * n_row
    me = frame * n_row + row
    last = sections - 1
    pending = []

    def member(index):
        return (seg, index // n_row, index % n_row)

    def remote(source, target, sem, device):
        return pltpu.make_async_remote_copy(
            src_ref=source,
            dst_ref=target,
            send_sem=send_sem.at[sem],
            recv_sem=recv_sem.at[sem],
            device_id=device,
            device_id_type=MESH,
        )

    def start_if(condition, copy):
        @pl.when(condition)
        def _():
            copy.start()

        pending.append((condition, copy))

    barrier = pltpu.get_barrier_semaphore()

    def greet(device):
        pl.semaphore_signal(barrier, inc=1, device_id=device, device_id_type=MESH)

    for step in range(1, peers):
        greet(member((me + step) % peers))

    @pl.when(seg > 0)
    def _():
        greet((seg - 1, frame, row))

    @pl.when(seg < last)
    def _():
        greet((seg + 1, frame, row))

    @pl.when((seg == 0) | (seg == last))
    def _():
        greet((last - seg, frame, row))

    linked = (seg > 0).astype(jnp.int32) + (seg < last).astype(jnp.int32)
    linked = linked + ((seg == 0) | (seg == last)).astype(jnp.int32)
    pl.semaphore_wait(barrier, peers - 1 + linked)

    after = (jnp.minimum(seg + 1, last), frame, row)
    before = (jnp.maximum(seg - 1, 0), frame, row)
    far = (last - seg, frame, row)
    x_copy = remote(x_out, x_in, 0, after)
    skip_copy = remote(x_out, skip_in, 1, far)
    u_copy = remote(u_out, u_in, 10, before)
    u_skip_copy = remote(u_out, u_skip, 11, far)

    def halo_start(padded, sem, index, size, at):
        onward = remote(
            padded.at[pl.ds(2 * BLOCK, BLOCK)], padded.at[pl.ds(0, BLOCK)],
            sem, at(jnp.minimum(index + 1, size - 1)),
        )
        back = remote(
            padded.at[pl.ds(BLOCK, BLOCK)], padded.at[pl.ds(3 * BLOCK, BLOCK)],
            sem + 1, at(jnp.maximum(index - 1, 0)),
        )
        start_if(index < size - 1, onward)
        start_if(index > 0, back)

        @pl.when(index == 0)
        def _():
            padded[pl.ds(0, BLOCK), :] = jnp.zeros((BLOCK, C), jnp.bfloat16)

        @pl.when(index == size - 1)
        def _():
            padded[pl.ds(3 * BLOCK, BLOCK), :] = jnp.zeros((BLOCK, C), jnp.bfloat16)

        return onward, back, index, size

    def halo_wait(started):
        onward, back, index, size = started

        @pl.when(index > 0)
        def _():
            onward.wait_recv()

        @pl.when(index < size - 1)
        def _():
            back.wait_recv()

    def row_start(padded, sem):
        return halo_start(padded, sem, row, n_row, lambda index: (seg, frame, index))

    def frame_start(padded, sem):
        return halo_start(padded, sem, frame, n_frame, lambda index: (seg, index, row))

    def exchange_start(turn, rows):
        stat_src[turn] = jnp.concatenate(rows + [jnp.zeros((8 - len(rows), C), jnp.float32)], axis=0)
        copies = []
        for step in range(1, peers):
            copy = remote(
                stat_src.at[turn], slots.at[turn, step - 1],
                12 + turn * (peers - 1) + step - 1, member((me + step) % peers),
            )
            copy.start()
            pending.append((None, copy))
            copies.append(copy)
        return turn, copies

    def exchange_wait(started):
        turn, copies = started
        total = stat_src[turn]
        for step, copy in enumerate(copies):
            copy.wait_recv()
            total = total + slots[turn, step]
        return total

    def column_sum(values):
        return jnp.sum(values.reshape(-1, C), axis=0, keepdims=True)

    def grouped(total):
        return lax.dot_general(
            total * inv_total[...], groups[...], (((1,), (0,)), ((), ())),
            precision=lax.Precision.HIGHEST, preferred_element_type=jnp.float32,
        )

    own = pl.ds(BLOCK, CELLS)

    @pl.when(seg == 0)
    def _():
        pad_x[own, :] = first_x[...]

    @pl.when(seg > 0)
    def _():
        x_copy.wait_recv()

    @pl.when((seg > 0) & (seg < last))
    def _():
        pad_x[own, :] = x_in[...]

    @pl.when(seg == last)
    def _():
        skip_copy.wait_recv()
        joined = x_in[...].astype(jnp.float32) + skip_in[...].astype(jnp.float32)
        pad_x[own, :] = joined.astype(jnp.bfloat16)

    halo_wait(row_start(pad_x, 2))
    widen(pad_x, wide_x)
    hidden = jnp.zeros((CELLS, C), jnp.float32)
    for a in range(3):
        for b in range(3):
            hidden = hidden + dot_nn(wide_x[b, pl.ds(a * BLOCK, CELLS), :], kernel[3 * a + b])
    normed[...] = hidden.reshape(normed.shape)
    rows = []
    for clip in range(CLIPS):
        part = normed[:, clip] + bias[pl.ds(clip, 1), :].reshape(1, 1, C)
        normed[:, clip] = part
        masked = part * mask[:, clip]
        rows += [column_sum(masked), column_sum(masked * part)]
    stats = exchange_start(0, rows)
    for b in range(3):
        x_turned[b] = jnp.transpose(wide_x[b], (1, 0))
    stats = grouped(exchange_wait(stats))
    inverses = []
    for clip in range(CLIPS):
        mean = stats[2 * clip : 2 * clip + 1]
        variance = stats[2 * clip + 1 : 2 * clip + 2] - mean * mean
        inverse = lax.rsqrt(variance + EPSILON)
        inverses.append(inverse)
        part = (normed[:, clip] - mean.reshape(1, 1, C)) * inverse.reshape(1, 1, C)
        normed[:, clip] = part
        scaled = part * gain[...].reshape(1, 1, C)
        grads[:, clip] = mask[:, clip] * (scaled * jax.nn.sigmoid(scaled))
    pad_a[own, :] = swap_order(grads[...].reshape(CELLS, C)).astype(jnp.bfloat16)
    halo_wait(frame_start(pad_a, 4))
    temporal = jnp.zeros((CELLS, C), jnp.float32)
    for k in range(3):
        temporal = temporal + dot_nn(pad_a[pl.ds(k * BLOCK, CELLS), :], tkernel[k])

    @pl.when(seg < last)
    def _():
        x_out[...] = (pad_x[own, :].astype(jnp.float32) + swap_order(temporal)).astype(jnp.bfloat16)

    start_if(seg < last, x_copy)
    start_if(seg == 0, skip_copy)
    a_turned[...] = jnp.transpose(pad_a[...], (1, 0))

    @pl.when(seg == last)
    def _():
        pad_u[own, :] = swap_order(last_up[...])

    @pl.when(seg < last)
    def _():
        u_copy.wait_recv()

    @pl.when((seg > 0) & (seg < last))
    def _():
        pad_u[own, :] = swap_order(u_in[...])

    @pl.when(seg == 0)
    def _():
        u_skip_copy.wait_recv()
        joined = u_in[...].astype(jnp.float32) + u_skip[...].astype(jnp.float32)
        pad_u[own, :] = swap_order(joined.astype(jnp.bfloat16))

    halo_wait(frame_start(pad_u, 6))
    act_grad = jnp.zeros((CELLS, C), jnp.float32)
    for k in range(3):
        act_grad = act_grad + dot_nt(pad_u[pl.ds((2 - k) * BLOCK, CELLS), :], tkernel[k])
    grads[...] = swap_order(act_grad).reshape(grads.shape)
    rows = []
    gain_part = jnp.zeros((1, C), jnp.float32)
    for clip in range(CLIPS):
        part = normed[:, clip]
        scaled = part * gain[...].reshape(1, 1, C)
        gate = jax.nn.sigmoid(scaled)
        scaled_grad = grads[:, clip] * mask[:, clip] * gate * (1.0 + scaled * (1.0 - gate))
        gain_part = gain_part + column_sum(scaled_grad * part)
        normed_grad = scaled_grad * gain[...].reshape(1, 1, C)
        grads[:, clip] = normed_grad
        rows += [column_sum(normed_grad), column_sum(normed_grad * part)]
    moments = exchange_start(1, rows)
    for k in range(3):
        temporal_out[k] = dot_nn(a_turned[:, pl.ds(k * BLOCK, CELLS)], pad_u[own, :])
    moments = grouped(exchange_wait(moments))
    rows = []
    for clip in range(CLIPS):
        first = moments[2 * clip : 2 * clip + 1].reshape(1, 1, C)
        second = moments[2 * clip + 1 : 2 * clip + 2].reshape(1, 1, C)
        part = inverses[clip].reshape(1, 1, C) * (
            grads[:, clip] - mask[:, clip] * (first + normed[:, clip] * second)
        )
        part = part.astype(jnp.bfloat16).astype(jnp.float32)
        grads[:, clip] = part
        rows.append(column_sum(part))
    pad_h[own, :] = grads[...].reshape(CELLS, C).astype(jnp.bfloat16)
    sums = exchange_start(2, rows + [gain_part])

    @pl.when(seg > 0)
    def _():
        halo = []
        pending_before = len(pending)
        halo = row_start(pad_h, 8)
        halo_wait(halo)
        widen(pad_h, wide_h)
        back = jnp.zeros((CELLS, C), jnp.float32)
        for a in range(3):
            for b in range(3):
                back = back + dot_nt(
                    wide_h[2 - b, pl.ds((2 - a) * BLOCK, CELLS), :], kernel[3 * a + b]
                )
        upstream = swap_order(pad_u[own, :]).astype(jnp.float32)
        u_out[...] = (upstream + back * width_mask[...]).astype(jnp.bfloat16)
        u_copy.start()
        for condition, copy in pending[pending_before:]:
            pl.when(condition)(copy.wait_send)
        del pending[pending_before:]

    @pl.when(seg == last)
    def _():
        u_skip_copy.start()

    for a in range(3):
        for b in range(3):
            spatial_out[3 * a + b] = dot_nn(
                x_turned[b, :, pl.ds(a * BLOCK, CELLS)], pad_h[own, :]
            )
    sums_out[...] = exchange_wait(sums)
    for condition, copy in pending + [(seg > 0, u_copy), (seg == last, u_skip_copy)]:
        if condition is None:
            copy.wait_send()
        else:
            pl.when(condition)(copy.wait_send)


def run_section(sections, n_frame, n_row, *operands):
    peers = n_frame * n_row
    flat = pltpu.VMEM((CELLS, C), jnp.bfloat16)
    padded = pltpu.VMEM((2 * CELLS, C), jnp.bfloat16)
    field = pltpu.VMEM((R_DEV * F_DEV, CLIPS, PAD, C), jnp.float32)
    sems = 12 + 3 * (peers - 1)
    vmem = pl.BlockSpec(memory_space=pltpu.VMEM)
    return pl.pallas_call(
        functools.partial(section_kernel, sections, n_frame, n_row),
        out_shape=(
            jax.ShapeDtypeStruct((9, C, C), jnp.float32),
            jax.ShapeDtypeStruct((3, C, C), jnp.float32),
            jax.ShapeDtypeStruct((8, C), jnp.float32),
        ),
        in_specs=[vmem] * len(operands),
        out_specs=(vmem, vmem, vmem),
        scratch_shapes=[flat] * 6
        + [padded] * 4
        + [pltpu.VMEM((3, 2 * CELLS, C), jnp.bfloat16)] * 2
        + [
            pltpu.VMEM((3, C, 2 * CELLS), jnp.bfloat16),
            pltpu.VMEM((C, 2 * CELLS), jnp.bfloat16),
            field,
            field,
            pltpu.VMEM((3, 8, C), jnp.float32),
            pltpu.VMEM((3, peers - 1, 8, C), jnp.float32),
            pltpu.SemaphoreType.DMA((sems,)),
            pltpu.SemaphoreType.DMA((sems,)),
        ],
        compiler_params=pltpu.CompilerParams(
            collective_id=0, has_side_effects=True, vmem_limit_bytes=48 * 1024 * 1024
        ),
    )(*operands)


def to_cells(array):
    turned = jnp.transpose(array, (2, 1, 0, 3, 4))
    turned = jnp.pad(turned, ((0, 0), (0, 0), (0, 0), (0, PAD - WIDTH), (0, 0)))
    return turned.reshape(CELLS, C)


def per_device(
    latents,
    cotangent,
    timesteps,
    frame_counts,
    spatial_weight,
    temporal_weight,
    time_weight,
    norm_gain,
):
    sections = lax.axis_size("segment")
    n_frame = lax.axis_size("frame")
    n_row = lax.axis_size("row")
    peers = n_frame * n_row
    me = lax.axis_index("frame") * n_row + lax.axis_index("row")
    group_width = C // G
    time_embed = time_features(timesteps)
    biases = jnp.dot(time_embed, time_weight[0], preferred_element_type=jnp.float32)
    frame_ids = lax.axis_index("frame") * F_DEV + jnp.arange(F_DEV)
    frame_mask = (frame_ids[None, :] < frame_counts[:, None]).astype(jnp.float32)
    upstream = (frame_mask[:, :, None, None, None] * cotangent.astype(jnp.float32)).astype(jnp.bfloat16)
    inside = (jnp.arange(PAD) < WIDTH).astype(jnp.float32)
    cell_mask = frame_mask.T[None, :, :, None] * inside
    cell_mask = jnp.broadcast_to(cell_mask, (R_DEV, F_DEV, CLIPS, PAD))
    width_mask = jnp.broadcast_to(inside, (R_DEV, F_DEV, CLIPS, PAD)).reshape(CELLS, 1)
    totals = frame_counts.astype(jnp.float32) * (R_DEV * n_row) * WIDTH * group_width
    inv_total = jnp.pad(jnp.repeat(1.0 / totals, 2), (0, 8 - 2 * CLIPS))[:, None]
    channel_group = jnp.arange(C) // group_width
    groups = (channel_group[:, None] == channel_group[None, :]).astype(jnp.float32)
    spatial, temporal, sums = run_section(
        sections,
        n_frame,
        n_row,
        to_cells(latents),
        to_cells(upstream),
        biases,
        cell_mask.reshape(R_DEV * F_DEV, CLIPS, PAD, 1),
        width_mask,
        inv_total,
        spatial_weight[0],
        temporal_weight[0],
        norm_gain,
        groups,
    )
    parts = jnp.concatenate(
        [spatial.reshape(peers, -1, C), temporal.reshape(peers, -1, C)], axis=1
    ).astype(jnp.bfloat16)
    reduced = lax.psum_scatter(parts, ("frame", "row"), scatter_dimension=0, tiled=True)[0]
    reduced = reduced.astype(jnp.float32)
    spatial_rows = 9 * C // peers
    time_rows = TE // peers
    embed = lax.dynamic_slice_in_dim(time_embed, me * time_rows, time_rows, 1).astype(jnp.float32)
    time_out = embed[0][:, None] * sums[0][None, :]
    for clip in range(1, CLIPS):
        time_out = time_out + embed[clip][:, None] * sums[clip][None, :]
    gain_out = lax.dynamic_slice_in_dim(sums[CLIPS], me * (C // peers), C // peers, 0)
    return (reduced[:spatial_rows][None], reduced[spatial_rows:][None], time_out[None], gain_out[None])


def solution(mesh):
    return jax.shard_map(
        per_device,
        mesh=mesh,
        in_specs=(
            P(None, "frame", "row", None, None),
            P(None, "frame", "row", None, None),
            P(),
            P(),
            P("segment", None, None, None),
            P("segment", None, None, None),
            P("segment", None, None),
            P("segment", None),
        ),
        out_specs=(
            P("segment", ("frame", "row"), None),
            P("segment", ("frame", "row"), None),
            P("segment", ("frame", "row"), None),
            P("segment", ("frame", "row")),
        ),
        check_vma=False,
    )
```

time: 684 us -> 246 us (0.36)
  blocking collectives: 159 us -> 0 us
  Pallas kernels: 0 us -> 139 us
  waiting for transfers between devices: 182 us -> 53.4 us
  starting transfers between devices: 123 us -> 0.04 us
  local copies, waits for them, and re-layouts: 81.5 us -> 23 us
  matrix products: 53.3 us -> 0.28 us
  other arithmetic: 55.8 us -> 15.3 us
  between operations: 24.8 us -> 14.2 us
    psum x10 -> x0, blocking collectives: 159 us -> none  [the longest x5 80.2 us: per_device(): lax.psum((group_sum(masked), group_sum(masked * hidden)), ('frame', 'row'))]
    pallas_call x0 -> x1, Pallas kernels: none -> 139 us  [run_section(): pl.pallas_call(functools.partial(section_kernel, sections, n_frame, n_row...]
    ppermute x50 -> x0, starting transfers between devices: 123 us -> none  [the longest x19 69 us: with_halo(): before = lax.ppermute(last, axis, up)]
    unnamed x3 -> x1, waiting for transfers between devices: 109 us -> 0.02 us
    dot_general x28 -> x0, matrix products: 53 us -> none  [the longest x18 33.7 us: flat_dot(): jnp.dot(columns.reshape(-1, matrix.shape[0]), matrix, preferred_element_t...]
    ppermute x50 -> x0, waiting for transfers between devices: 27.1 us -> none  [the longest x12 22.7 us: shifted(): return lax.ppermute(array, axis, pairs)]
    concatenate x14 -> x0, local copies, waits for them, and re-layouts: 26.2 us -> none  [the longest x10 18.5 us: spatial_columns(): jnp.concatenate([padded[:, vertical:vertical + row_count, lateral:lateral...]
    convert_element_type x15 -> x4, other arithmetic: 13.3 us -> 2.42 us  [the longest x1 0.87 us: per_device(): (channel_group[:, None] == channel_group[None, :]).astype(jnp.float32)]
  transfers between devices with their start and end apart: 52 -> 1, of which waited for: 16 -> 1; matrix products, arithmetic and copies ran while one was open for 22% -> 1% of each run, Pallas kernels for 0% -> 0%
where the time goes in v1:
time: 246 us; the launch traced here: 245 us
  Pallas kernels  139 us (57%)
  waiting for transfers between devices  53.4 us (22%)
  local copies, waits for them, and re-layouts  23 us (9%)
  other arithmetic  15.3 us (6%)
  between operations  14.2 us (6%)
    pallas_call x1, Pallas kernels, run_section(): pl.pallas_call(functools.partial(section_kernel, sections, n_frame, n_row...  139 us
    reduce_scatter x1, waiting for transfers between devices, per_device(): lax.psum_scatter(parts, ('frame', 'row'), scatter_dimension=0, tiled=True)  53.3 us
    unnamed x20, local copies, waits for them, and re-layouts  5.15 us
  transfers between devices with their start and end apart: 1, of which 1 were waited for; matrix products, arithmetic and copies ran while one was open for 1% of the time, Pallas kernels for 0%

profile of v1, /device:TPU:0, one launch (start us, length us, event | category | flops | bytes accessed | tf_op | source)
XLA Modules:
  0.0 245.4 jit_solution(3459107512655451562)
XLA Ops:
  7.2 0.0 copy-start
  7.2 0.0 copy-start.1
  7.2 0.0 reduce-scatter.2.cloned.1.call-start
  7.2 0.6 multiply_exponential_fusion
  7.8 0.0 copy-start.8
  7.8 0.6 add_select_fusion
  8.5 0.9 copy.24
  9.4 1.2 multiply_divide_fusion
  10.6 0.8 compare_convert_fusion.2
  11.4 1.0 fusion.2
  12.5 1.2 convert_element_type.64
  13.7 0.1 broadcast_multiply_fusion
  13.7 0.6 broadcast_in_dim.8
  14.3 0.0 copy-done.8
  14.3 0.8 copy.19.mask
  15.1 1.2 broadcast_in_dim.9
  16.4 1.5 reshape.257.width_mask
  17.9 1.3 broadcast_in_dim.10
  19.1 1.3 reshape.254
  20.4 1.2 pad_bitcast_fusion
  21.6 1.3 copy.21.inv_total
  22.9 0.9 compare_convert_fusion.groups
  23.8 0.8 multiply_cosine_fusion
  24.7 0.0 copy-done
  24.7 0.0 copy-start.7
  24.7 0.3 fusion.bias
  25.0 0.3 copy-done.7
  25.3 0.0 copy-done.1
  25.3 1.1 copy-done.2
  26.4 0.9 copy-done.3
  27.3 0.7 copy-done.4
  28.0 0.7 copy-done.6
  28.7 139.3 %shard_map.111 = (f32[9,320,320]{2,1,0:T(8,128)}, f32[3,320,320]{2,1,0:T(8,128)S(1)}, f32[8,320]{1,0:T(8,128)S(1)}) custom-call(bf16[256,320]{1,0:T(8,128)(2,1)S(1)} %bitcast.19, bf16[256,320]{1,0:T(8,128)(2,1)S(1)} %bitcast.20, f32[2,320]{1,0:T(2,128)S(1)} %fusion.bias, f32[4,2,32,1]{3,2,1,0:T(8,128)S(1)} %copy.19.mask, f32[256,1]{1,0:T(8,128)S(1)} %copy-done.3, ...), custom_call_target="tpu_custom_call" | custom-call | tf_op jit(solution)/shard_map/pallas_call | solution.py:352
  168.0 0.0 copy-start.5
  168.0 0.1 convert.9
  168.1 0.5 copy-done.5
  168.6 1.1 copy.23
  169.7 2.5 %convert.8 = bf16[9,320,320]{2,1,0:T(8,128)(2,1)S(1)} convert(f32[9,320,320]{2,1,0:T(8,128)} %get-tuple-element.7) | non-fusion elementwise | flops 921600 | bytes 5529600 | tf_op jit(solution)/shard_map/convert.3
  172.2 2.6 %copy.22 = bf16[8,360,320]{1,2,0:T(8,128)(2,1)} copy(bf16[8,360,320]{2,1,0:T(8,128)(2,1)S(1)} %bitcast.22) | data formatting | bytes 3686400 | tf_op jit(solution)/shard_map/reshape | solution.py:431
  174.9 3.9 %pad_maximum_fusion = bf16[8,480,320]{1,2,0:T(8,128)(2,1)} fusion(bf16[8,120,320]{1,2,0:T(8,128)(2,1)} %copy.23, bf16[8,360,320]{1,2,0:T(8,128)(2,1)} %copy.22), kind=kLoop, calls=%fused_computation | loop fusion | flops 4915200 | bytes 4915200 | tf_op jit(solution)/shard_map/concatenate | solution.py:430
  178.8 0.0 reduce-scatter.2.cloned.1.call-update
  178.8 0.8 slice_reduce_fusion.1
  179.6 0.6 constant_dynamic-slice_fusion
  180.2 0.8 dynamic-slice_convert_fusion
  181.0 0.8 multiply_add_fusion
  181.8 53.3 %reduce-scatter.2.cloned.1.call-done = bf16[1,480,320]{1,2,0:T(8,128)(2,1)} async-done(((bf16[8,480,320]{1,2,0:T(8,128)(2,1)}), bf16[1,480,320]{1,2,0:T(8,128)(2,1)}) %reduce-scatter.2.cloned.1.call-update) | async-done | bytes 307216 | tf_op jit(solution)/shard_map/reduce_scatter | solution.py:433
  235.1 1.8 slice.36
  236.9 1.7 slice.37
  (11 shorter events, 0.1 us)
Async XLA Ops:
  7.2 17.5 %copy-start = (bf16[1,1280,320]{1,2,0:T(8,128)(2,1)S(1)}, bf16[1,1280,320]{1,2,0:T(8,128)(2,1)}, u32[]{:S(2)}) copy-start(bf16[1,1280,320]{1,2,0:T(8,128)(2,1)} %param.14) | copy-start | bytes 2457604
  7.2 18.1 %copy-start.1 = (bf16[1,9,320,320]{3,2,1,0:T(8,128)(2,1)S(1)}, bf16[1,9,320,320]{3,2,1,0:T(8,128)(2,1)}, u32[]{:S(2)}) copy-start(bf16[1,9,320,320]{3,2,1,0:T(8,128)(2,1)} %param.12) | copy-start | bytes 5529604
  7.2 227.9 %reduce-scatter.2.cloned.1.call-start = ((), (), s32[]{:S(2)}) async-start(), calls=%async_computation.1 | async-start | bytes 2949120 | tf_op jit(solution)/shard_map/reduce_scatter | solution.py:433
  7.8 6.5 %copy-start.8 = (f32[32]{0:T(128)}, f32[32]{0:T(128)S(1)}, u32[]{:S(2)}) copy-start(f32[32]{0:T(128)S(1)} %compare_convert_fusion.1) | copy-start | bytes 388
  24.7 0.6 copy-start.7
  25.3 1.1 copy-start.2
  26.4 0.9 copy-start.3
  27.3 0.7 copy-start.4
  28.0 0.7 copy-start.6
  168.0 0.6 copy-start.5
Sparse Core Ops, SparseCore 0:
  178.9 56.1 reduce-scatter.1

commit v2 on v1

--- a/solution.py
+++ b/solution.py
@@ -59,10 +59,11 @@
 
 def section_kernel(
     sections, n_frame, n_row,
-    first_x, last_up, bias, mask, width_mask, inv_total, kernel, tkernel, gain, groups,
+    counts, latents, cotangent, embed, kernel, tkernel, time_kernel, gain,
     spatial_out, temporal_out, sums_out,
     x_in, skip_in, x_out, u_in, u_skip, u_out, pad_x, pad_a, pad_u, pad_h, wide_x, wide_h,
-    x_turned, a_turned, normed, grads, stat_src, slots, send_sem, recv_sem,
+    x_turned, a_turned, normed, grads, stat_src, slots, mask, width_mask, groups, bias,
+    send_sem, recv_sem, *reduction,
 ):
     seg = lax.axis_index("segment")
     frame = lax.axis_index("frame")
@@ -91,6 +92,21 @@
             copy.start()
 
         pending.append((condition, copy))
+
+    place = lax.broadcasted_iota(jnp.int32, (R_DEV * F_DEV, PAD, 1), 0) % F_DEV + frame * F_DEV
+    column = lax.broadcasted_iota(jnp.int32, (R_DEV * F_DEV, PAD, 1), 1)
+    for clip in range(CLIPS):
+        live = (place < counts[clip]) & (column < WIDTH)
+        mask[:, clip] = jnp.where(live, 1.0, 0.0)
+    column = lax.broadcasted_iota(jnp.int32, (CELLS // PAD, PAD, 1), 1)
+    width_mask[...] = jnp.where(column < WIDTH, 1.0, 0.0).reshape(CELLS, 1)
+    ids = [lax.broadcasted_iota(jnp.int32, (C, C), dim).astype(jnp.float32) for dim in range(2)]
+    ids = [jnp.floor((one + 0.5) * (G / C)) for one in ids]
+    groups[...] = jnp.where(ids[0] == ids[1], 1.0, 0.0)
+    bias[...] = dot_nn(embed[...], time_kernel[...])
+    line = lax.broadcasted_iota(jnp.int32, (8, C), 0)
+    in_use = jnp.where(line < 2, counts[0], counts[1]).astype(jnp.float32)
+    inv_total = 1.0 / (in_use * (R_DEV * n_row * WIDTH * (C // G)))
 
     barrier = pltpu.get_barrier_semaphore()
 
@@ -189,15 +205,69 @@
 
     def grouped(total):
         return lax.dot_general(
-            total * inv_total[...], groups[...], (((1,), (0,)), ((), ())),
+            total * inv_total, groups[...], (((1,), (0,)), ((), ())),
             precision=lax.Precision.HIGHEST, preferred_element_type=jnp.float32,
         )
 
+    fused = bool(reduction)
+    temporal_sum, spatial_sum = reduction[:2] if fused else (temporal_out, spatial_out)
+    first_sem = 12 + 3 * (peers - 1)
+
+    def stage(total, buffers):
+        staged = buffers[0]
+        rows = total.shape[0] // peers
+        for index in range(peers):
+            staged[index, :rows] = total[pl.ds(index * rows, rows), :].astype(jnp.bfloat16)
+            if rows < staged.shape[1]:
+                rest = staged.shape[1] - rows
+                staged[index, rows:] = jnp.zeros((rest, C), jnp.bfloat16)
+
+    def pair_start(buffers, turn):
+        staged, landed = buffers[:2]
+        other = 1 - frame
+        copy = remote(
+            staged.at[pl.ds(other * n_row, n_row)], landed,
+            first_sem + turn * n_row, (seg, other, row),
+        )
+        copy.start()
+        pending.append((None, copy))
+        return copy
+
+    def line_start(buffers, turn, pair):
+        staged, landed, added, arrived = buffers
+        pair.wait_recv()
+        copies = []
+        for step in range(n_row - 1, 0, -1):
+            target = (row + step) % n_row
+            mine = staged[frame * n_row + target].astype(jnp.float32)
+            added[target] = (mine + landed[target].astype(jnp.float32)).astype(jnp.bfloat16)
+            copy = remote(
+                added.at[target], arrived.at[step - 1],
+                first_sem + turn * n_row + step, (seg, frame, target),
+            )
+            copy.start()
+            pending.append((None, copy))
+            copies.append((step, copy))
+        return copies
+
+    def line_finish(buffers, copies, result):
+        staged, landed, added, arrived = buffers
+        total = staged[frame * n_row + row].astype(jnp.float32) + landed[row].astype(jnp.float32)
+        for step, copy in copies:
+            copy.wait_recv()
+            total = total + arrived[step - 1].astype(jnp.float32)
+        result[...] = total[: result.shape[0]]
+
     own = pl.ds(BLOCK, CELLS)
 
     @pl.when(seg == 0)
     def _():
-        pad_x[own, :] = first_x[...]
+        pad_x[own, :] = jnp.zeros((CELLS, C), jnp.bfloat16)
+        for r in range(R_DEV):
+            for f in range(F_DEV):
+                for clip in range(CLIPS):
+                    start = BLOCK + ((r * F_DEV + f) * CLIPS + clip) * PAD
+                    pad_x[pl.ds(start, WIDTH), :] = latents[clip, f, r]
 
     @pl.when(seg > 0)
     def _():
@@ -256,7 +326,14 @@
 
     @pl.when(seg == last)
     def _():
-        pad_u[own, :] = swap_order(last_up[...])
+        pad_u[own, :] = jnp.zeros((CELLS, C), jnp.bfloat16)
+        for r in range(R_DEV):
+            for f in range(F_DEV):
+                for clip in range(CLIPS):
+                    start = BLOCK + ((f * R_DEV + r) * CLIPS + clip) * PAD
+                    kept = mask[r * F_DEV + f, clip][:WIDTH]
+                    value = kept * cotangent[clip, f, r].astype(jnp.float32)
+                    pad_u[pl.ds(start, WIDTH), :] = value.astype(jnp.bfloat16)
 
     @pl.when(seg < last)
     def _():
@@ -290,8 +367,14 @@
         rows += [column_sum(normed_grad), column_sum(normed_grad * part)]
     moments = exchange_start(1, rows)
     for k in range(3):
-        temporal_out[k] = dot_nn(a_turned[:, pl.ds(k * BLOCK, CELLS)], pad_u[own, :])
+        temporal_sum[pl.ds(k * C, C), :] = dot_nn(
+            a_turned[:, pl.ds(k * BLOCK, CELLS)], pad_u[own, :]
+        )
+    if fused:
+        stage(temporal_sum, reduction[2:6])
     moments = grouped(exchange_wait(moments))
+    if fused:
+        temporal_pair = pair_start(reduction[2:6], 0)
     rows = []
     for clip in range(CLIPS):
         first = moments[2 * clip : 2 * clip + 1].reshape(1, 1, C)
@@ -329,11 +412,18 @@
     def _():
         u_skip_copy.start()
 
+    if fused:
+        temporal_line = line_start(reduction[2:6], 0, temporal_pair)
     for a in range(3):
         for b in range(3):
-            spatial_out[3 * a + b] = dot_nn(
+            spatial_sum[pl.ds((3 * a + b) * C, C), :] = dot_nn(
                 x_turned[b, :, pl.ds(a * BLOCK, CELLS)], pad_h[own, :]
             )
+    if fused:
+        stage(spatial_sum, reduction[6:10])
+        spatial_line = line_start(reduction[6:10], 1, pair_start(reduction[6:10], 1))
+        line_finish(reduction[2:6], temporal_line, temporal_out)
+        line_finish(reduction[6:10], spatial_line, spatial_out)
     sums_out[...] = exchange_wait(sums)
     for condition, copy in pending + [(seg > 0, u_copy), (seg == last, u_skip_copy)]:
         if condition is None:
@@ -344,19 +434,31 @@
 
 def run_section(sections, n_frame, n_row, *operands):
     peers = n_frame * n_row
+    fused = n_frame == 2 and C * 3 % (8 * peers) == 0
     flat = pltpu.VMEM((CELLS, C), jnp.bfloat16)
     padded = pltpu.VMEM((2 * CELLS, C), jnp.bfloat16)
     field = pltpu.VMEM((R_DEV * F_DEV, CLIPS, PAD, C), jnp.float32)
-    sems = 12 + 3 * (peers - 1)
+    sems = 12 + 3 * (peers - 1) + 2 * n_row
     vmem = pl.BlockSpec(memory_space=pltpu.VMEM)
+    smem = pl.BlockSpec(memory_space=pltpu.SMEM)
+    taps = (3, 9)
+    share = peers if fused else 1
+    reduction = []
+    if fused:
+        reduction = [pltpu.VMEM((count * C, C), jnp.float32) for count in taps]
+        for count in taps:
+            rows = -(-count * C // (16 * peers)) * 16
+            reduction += [
+                pltpu.VMEM((held, rows, C), jnp.bfloat16) for held in (peers, n_row, n_row, n_row - 1)
+            ]
     return pl.pallas_call(
         functools.partial(section_kernel, sections, n_frame, n_row),
         out_shape=(
-            jax.ShapeDtypeStruct((9, C, C), jnp.float32),
-            jax.ShapeDtypeStruct((3, C, C), jnp.float32),
+            jax.ShapeDtypeStruct((9 * C // share, C), jnp.float32),
+            jax.ShapeDtypeStruct((3 * C // share, C), jnp.float32),
             jax.ShapeDtypeStruct((8, C), jnp.float32),
         ),
-        in_specs=[vmem] * len(operands),
+        in_specs=[smem] + [vmem] * (len(operands) - 1),
         out_specs=(vmem, vmem, vmem),
         scratch_shapes=[flat] * 6
         + [padded] * 4
@@ -368,19 +470,18 @@
             field,
             pltpu.VMEM((3, 8, C), jnp.float32),
             pltpu.VMEM((3, peers - 1, 8, C), jnp.float32),
+            pltpu.VMEM((R_DEV * F_DEV, CLIPS, PAD, 1), jnp.float32),
+            pltpu.VMEM((CELLS, 1), jnp.float32),
+            pltpu.VMEM((C, C), jnp.float32),
+            pltpu.VMEM((16, C), jnp.float32),
             pltpu.SemaphoreType.DMA((sems,)),
             pltpu.SemaphoreType.DMA((sems,)),
-        ],
+        ]
+        + reduction,
         compiler_params=pltpu.CompilerParams(
-            collective_id=0, has_side_effects=True, vmem_limit_bytes=48 * 1024 * 1024
+            collective_id=0, has_side_effects=True, vmem_limit_bytes=56 * 1024 * 1024
         ),
     )(*operands)
-
-
-def to_cells(array):
-    turned = jnp.transpose(array, (2, 1, 0, 3, 4))
-    turned = jnp.pad(turned, ((0, 0), (0, 0), (0, 0), (0, PAD - WIDTH), (0, 0)))
-    return turned.reshape(CELLS, C)
 
 
 def per_device(
@@ -398,48 +499,33 @@
     n_row = lax.axis_size("row")
     peers = n_frame * n_row
     me = lax.axis_index("frame") * n_row + lax.axis_index("row")
-    group_width = C // G
-    time_embed = time_features(timesteps)
-    biases = jnp.dot(time_embed, time_weight[0], preferred_element_type=jnp.float32)
-    frame_ids = lax.axis_index("frame") * F_DEV + jnp.arange(F_DEV)
-    frame_mask = (frame_ids[None, :] < frame_counts[:, None]).astype(jnp.float32)
-    upstream = (frame_mask[:, :, None, None, None] * cotangent.astype(jnp.float32)).astype(jnp.bfloat16)
-    inside = (jnp.arange(PAD) < WIDTH).astype(jnp.float32)
-    cell_mask = frame_mask.T[None, :, :, None] * inside
-    cell_mask = jnp.broadcast_to(cell_mask, (R_DEV, F_DEV, CLIPS, PAD))
-    width_mask = jnp.broadcast_to(inside, (R_DEV, F_DEV, CLIPS, PAD)).reshape(CELLS, 1)
-    totals = frame_counts.astype(jnp.float32) * (R_DEV * n_row) * WIDTH * group_width
-    inv_total = jnp.pad(jnp.repeat(1.0 / totals, 2), (0, 8 - 2 * CLIPS))[:, None]
-    channel_group = jnp.arange(C) // group_width
-    groups = (channel_group[:, None] == channel_group[None, :]).astype(jnp.float32)
+    time_embed = time_features(jnp.pad(timesteps, (0, 16 - CLIPS)))
     spatial, temporal, sums = run_section(
         sections,
         n_frame,
         n_row,
-        to_cells(latents),
-        to_cells(upstream),
-        biases,
-        cell_mask.reshape(R_DEV * F_DEV, CLIPS, PAD, 1),
-        width_mask,
-        inv_total,
+        frame_counts,
+        latents,
+        cotangent,
+        time_embed,
         spatial_weight[0],
         temporal_weight[0],
+        time_weight[0],
         norm_gain,
-        groups,
     )
-    parts = jnp.concatenate(
-        [spatial.reshape(peers, -1, C), temporal.reshape(peers, -1, C)], axis=1
-    ).astype(jnp.bfloat16)
-    reduced = lax.psum_scatter(parts, ("frame", "row"), scatter_dimension=0, tiled=True)[0]
-    reduced = reduced.astype(jnp.float32)
-    spatial_rows = 9 * C // peers
+    if spatial.shape[0] == 9 * C:
+        parts = [spatial.reshape(peers, -1, C), temporal.reshape(peers, -1, C)]
+        parts = jnp.concatenate(parts, axis=1).astype(jnp.bfloat16)
+        reduced = lax.psum_scatter(parts, ("frame", "row"), scatter_dimension=0, tiled=True)[0]
+        reduced = reduced.astype(jnp.float32)
+        spatial, temporal = reduced[: 9 * C // peers], reduced[9 * C // peers :]
     time_rows = TE // peers
     embed = lax.dynamic_slice_in_dim(time_embed, me * time_rows, time_rows, 1).astype(jnp.float32)
     time_out = embed[0][:, None] * sums[0][None, :]
     for clip in range(1, CLIPS):
         time_out = time_out + embed[clip][:, None] * sums[clip][None, :]
     gain_out = lax.dynamic_slice_in_dim(sums[CLIPS], me * (C // peers), C // peers, 0)
-    return (reduced[:spatial_rows][None], reduced[spatial_rows:][None], time_out[None], gain_out[None])
+    return (spatial[None], temporal[None], time_out[None], gain_out[None])
 
 
 def solution(mesh):

time: 246 us -> 185 us (0.75)
  waiting for transfers between devices: 53.4 us -> 0 us
  Pallas kernels: 139 us -> 173 us
  local copies, waits for them, and re-layouts: 23 us -> 7.39 us
  between operations: 14.2 us -> 0.66 us
  other arithmetic: 15.3 us -> 3.14 us
    reduce_scatter x1 -> x0, waiting for transfers between devices: 53.3 us -> none  [per_device(): lax.psum_scatter(parts, ('frame', 'row'), scatter_dimension=0, tiled=True)]
    pallas_call x1, Pallas kernels: 139 us -> 173 us  [run_section(): pl.pallas_call(functools.partial(section_kernel, sections, n_frame, n_row...]
    reshape x5 -> x0, local copies, waits for them, and re-layouts: 7.34 us -> none  [the longest x1 2.62 us: per_device(): spatial.reshape(peers, -1, C)]
    broadcast_in_dim x5 -> x0, local copies, waits for them, and re-layouts: 5.58 us -> none  [the longest x2 2.48 us: per_device(): jnp.pad(jnp.repeat(1.0 / totals, 2), (0, 8 - 2 * CLIPS))[:, None]]
    concatenate x1 -> x0, other arithmetic: 3.9 us -> none  [per_device(): jnp.concatenate([spatial.reshape(peers, -1, C), temporal.reshape(peers, -...]
    slice x2 -> x0, local copies, waits for them, and re-layouts: 3.43 us -> none  [the longest x1 1.75 us: per_device(): reduced[:spatial_rows][None]]
    another operation x2 -> x0, other arithmetic: 2.6 us -> none
    unnamed x20 -> x3, local copies, waits for them, and re-layouts: 5.15 us -> 5.97 us
  transfers between devices with their start and end apart: 1 -> 0, of which waited for: 1 -> 0; matrix products, arithmetic and copies ran while one was open for 1% -> 0% of each run, Pallas kernels for 0% -> 0%
where the time goes in v2:
time: 185 us
  Pallas kernels  173 us (94%)
  local copies, waits for them, and re-layouts  7.39 us (4%)
  other arithmetic  3.14 us (2%)
    pallas_call x1, Pallas kernels, run_section(): pl.pallas_call(functools.partial(section_kernel, sections, n_frame, n_row...  173 us
    unnamed x3, local copies, waits for them, and re-layouts  5.97 us

profile of v2, /device:TPU:0, one launch (start us, length us, event | category | flops | bytes accessed | tf_op | source)
XLA Modules:
  0.0 184.5 jit_solution(1281671956249141021)
XLA Ops:
  0.6 0.7 pad_convert_fusion
  1.3 0.2 multiply_cosine_fusion
  1.5 0.7 multiply_convert_fusion.embed
  2.2 2.2 %copy.12 = bf16[1,1280,320]{2,1,0:T(8,128)(2,1)} copy(bf16[1,1280,320]{1,2,0:T(8,128)(2,1)} %param.14) | data formatting | bytes 1638400 | tf_op args[6]
  4.4 173.3 %shard_map.111 = (f32[360,320]{1,0:T(8,128)}, f32[120,320]{1,0:T(8,128)}, f32[8,320]{1,0:T(8,128)}) custom-call(s32[2]{0:T(128)} %counts.1, bf16[2,2,2,24,320]{4,3,2,1,0:T(8,128)(2,1)} %latents.1, bf16[2,2,2,24,320]{4,3,2,1,0:T(8,128)(2,1)} %cotangent.1, bf16[16,1280]{1,0:T(8,128)(2,1)} %multiply_convert_fusion.embed, bf16[9,320,320]{2,1,0:T(8,128)(2,1)} %bitcast.8, ...), custom_call_target="tpu_custom_call" | custom-call | tf_op jit(solution)/shard_map/pallas_call | solution.py:454
  177.7 2.0 %copy.13 = f32[1,360,320]{1,2,0:T(8,128)} copy(f32[1,360,320]{2,1,0:T(8,128)} %bitcast.10) | data formatting | bytes 921600
  179.8 1.7 copy.14
  181.5 0.8 slice_reduce_fusion.1
  182.3 0.8 dynamic-slice_convert_fusion
  183.1 0.8 multiply_add_fusion
  183.9 0.6 constant_dynamic-slice_fusion
  (2 shorter events, 0.0 us)

commit v3 on v2

--- a/solution.py
+++ b/solution.py
@@ -48,13 +48,13 @@
     return lax.dot_general(left, right, (((1,), (1,)), ((), ())), preferred_element_type=jnp.float32)
 
 
-def widen(padded, wide):
-    values = padded[...]
+def widen(padded, wide, start, length):
+    some = pl.ds(start, length)
+    values = padded[some, :]
     exact = values.astype(jnp.float32)
-    length = values.shape[0]
-    wide[0] = pltpu.roll(exact, 1, 0).astype(jnp.bfloat16)
-    wide[1] = values
-    wide[2] = pltpu.roll(exact, length - 1, 0).astype(jnp.bfloat16)
+    wide[0, some, :] = pltpu.roll(exact, 1, 0).astype(jnp.bfloat16)
+    wide[1, some, :] = values
+    wide[2, some, :] = pltpu.roll(exact, length - 1, 0).astype(jnp.bfloat16)
 
 
 def section_kernel(
@@ -258,6 +258,37 @@
             total = total + arrived[step - 1].astype(jnp.float32)
         result[...] = total[: result.shape[0]]
 
+    def spatial_pass(padded, wide, sem, term):
+        halo = row_start(padded, sem)
+        widen(padded, wide, BLOCK, CELLS)
+        total = term(1, 0) + term(1, 1) + term(1, 2)
+        halo_wait(halo)
+        widen(padded, wide, 0, BLOCK)
+        widen(padded, wide, 3 * BLOCK, BLOCK)
+        for a in (0, 2):
+            for b in range(3):
+                total = total + term(a, b)
+        return total
+
+    def temporal_pass(padded, sem, term):
+        halo = frame_start(padded, sem)
+        total = term(1)
+        halo_wait(halo)
+        return total + term(0) + term(2)
+
+    def turn():
+        for b in range(3):
+            x_turned[b] = jnp.transpose(wide_x[b], (1, 0))
+        a_turned[...] = jnp.transpose(pad_a[...], (1, 0))
+
+    def temporal_grad():
+        for k in range(3):
+            temporal_sum[pl.ds(k * C, C), :] = dot_nn(
+                a_turned[:, pl.ds(k * BLOCK, CELLS)], pad_u[own, :]
+            )
+        if fused:
+            stage(temporal_sum, reduction[2:6])
+
     own = pl.ds(BLOCK, CELLS)
 
     @pl.when(seg == 0)
@@ -283,12 +314,10 @@
         joined = x_in[...].astype(jnp.float32) + skip_in[...].astype(jnp.float32)
         pad_x[own, :] = joined.astype(jnp.bfloat16)
 
-    halo_wait(row_start(pad_x, 2))
-    widen(pad_x, wide_x)
-    hidden = jnp.zeros((CELLS, C), jnp.float32)
-    for a in range(3):
-        for b in range(3):
-            hidden = hidden + dot_nn(wide_x[b, pl.ds(a * BLOCK, CELLS), :], kernel[3 * a + b])
+    hidden = spatial_pass(
+        pad_x, wide_x, 2,
+        lambda a, b: dot_nn(wide_x[b, pl.ds(a * BLOCK, CELLS), :], kernel[3 * a + b]),
+    )
     normed[...] = hidden.reshape(normed.shape)
     rows = []
     for clip in range(CLIPS):
@@ -297,8 +326,6 @@
         masked = part * mask[:, clip]
         rows += [column_sum(masked), column_sum(masked * part)]
     stats = exchange_start(0, rows)
-    for b in range(3):
-        x_turned[b] = jnp.transpose(wide_x[b], (1, 0))
     stats = grouped(exchange_wait(stats))
     inverses = []
     for clip in range(CLIPS):
@@ -311,10 +338,9 @@
         scaled = part * gain[...].reshape(1, 1, C)
         grads[:, clip] = mask[:, clip] * (scaled * jax.nn.sigmoid(scaled))
     pad_a[own, :] = swap_order(grads[...].reshape(CELLS, C)).astype(jnp.bfloat16)
-    halo_wait(frame_start(pad_a, 4))
-    temporal = jnp.zeros((CELLS, C), jnp.float32)
-    for k in range(3):
-        temporal = temporal + dot_nn(pad_a[pl.ds(k * BLOCK, CELLS), :], tkernel[k])
+    temporal = temporal_pass(
+        pad_a, 4, lambda k: dot_nn(pad_a[pl.ds(k * BLOCK, CELLS), :], tkernel[k])
+    )
 
     @pl.when(seg < last)
     def _():
@@ -322,7 +348,7 @@
 
     start_if(seg < last, x_copy)
     start_if(seg == 0, skip_copy)
-    a_turned[...] = jnp.transpose(pad_a[...], (1, 0))
+    pl.when(seg < last)(turn)
 
     @pl.when(seg == last)
     def _():
@@ -349,10 +375,9 @@
         joined = u_in[...].astype(jnp.float32) + u_skip[...].astype(jnp.float32)
         pad_u[own, :] = swap_order(joined.astype(jnp.bfloat16))
 
-    halo_wait(frame_start(pad_u, 6))
-    act_grad = jnp.zeros((CELLS, C), jnp.float32)
-    for k in range(3):
-        act_grad = act_grad + dot_nt(pad_u[pl.ds((2 - k) * BLOCK, CELLS), :], tkernel[k])
+    act_grad = temporal_pass(
+        pad_u, 6, lambda k: dot_nt(pad_u[pl.ds(k * BLOCK, CELLS), :], tkernel[2 - k])
+    )
     grads[...] = swap_order(act_grad).reshape(grads.shape)
     rows = []
     gain_part = jnp.zeros((1, C), jnp.float32)
@@ -366,15 +391,8 @@
         grads[:, clip] = normed_grad
         rows += [column_sum(normed_grad), column_sum(normed_grad * part)]
     moments = exchange_start(1, rows)
-    for k in range(3):
-        temporal_sum[pl.ds(k * C, C), :] = dot_nn(
-            a_turned[:, pl.ds(k * BLOCK, CELLS)], pad_u[own, :]
-        )
-    if fused:
-        stage(temporal_sum, reduction[2:6])
+    pl.when(seg == 0)(temporal_grad)
     moments = grouped(exchange_wait(moments))
-    if fused:
-        temporal_pair = pair_start(reduction[2:6], 0)
     rows = []
     for clip in range(CLIPS):
         first = moments[2 * clip : 2 * clip + 1].reshape(1, 1, C)
@@ -386,21 +404,13 @@
         grads[:, clip] = part
         rows.append(column_sum(part))
     pad_h[own, :] = grads[...].reshape(CELLS, C).astype(jnp.bfloat16)
-    sums = exchange_start(2, rows + [gain_part])
-
     @pl.when(seg > 0)
     def _():
-        halo = []
         pending_before = len(pending)
-        halo = row_start(pad_h, 8)
-        halo_wait(halo)
-        widen(pad_h, wide_h)
-        back = jnp.zeros((CELLS, C), jnp.float32)
-        for a in range(3):
-            for b in range(3):
-                back = back + dot_nt(
-                    wide_h[2 - b, pl.ds((2 - a) * BLOCK, CELLS), :], kernel[3 * a + b]
-                )
+        back = spatial_pass(
+            pad_h, wide_h, 8,
+            lambda a, b: dot_nt(wide_h[b, pl.ds(a * BLOCK, CELLS), :], kernel[8 - 3 * a - b]),
+        )
         upstream = swap_order(pad_u[own, :]).astype(jnp.float32)
         u_out[...] = (upstream + back * width_mask[...]).astype(jnp.bfloat16)
         u_copy.start()
@@ -411,10 +421,15 @@
     @pl.when(seg == last)
     def _():
         u_skip_copy.start()
-
+        turn()
+
+    pl.when(seg > 0)(temporal_grad)
+    sums = exchange_start(2, rows + [gain_part])
     if fused:
-        temporal_line = line_start(reduction[2:6], 0, temporal_pair)
+        temporal_pair = pair_start(reduction[2:6], 0)
     for a in range(3):
+        if fused and a == 1:
+            temporal_line = line_start(reduction[2:6], 0, temporal_pair)
         for b in range(3):
             spatial_sum[pl.ds((3 * a + b) * C, C), :] = dot_nn(
                 x_turned[b, :, pl.ds(a * BLOCK, CELLS)], pad_h[own, :]

time: 185 us -> 177 us (0.957)
  Pallas kernels: 173 us -> 166 us
    pallas_call x1, Pallas kernels: 173 us -> 166 us  [run_section(): pl.pallas_call(functools.partial(section_kernel, sections, n_frame, n_row...]
where the time goes in v3:
time: 177 us
  Pallas kernels  166 us (94%)
  local copies, waits for them, and re-layouts  7.39 us (4%)
  other arithmetic  3.14 us (2%)
    pallas_call x1, Pallas kernels, run_section(): pl.pallas_call(functools.partial(section_kernel, sections, n_frame, n_row...  166 us
    unnamed x3, local copies, waits for them, and re-layouts  5.97 us

profile of v3, /device:TPU:0, one launch (start us, length us, event | category | flops | bytes accessed | tf_op | source)
XLA Modules:
  0.0 177.1 jit_solution(17639296053155258973)
XLA Ops:
  0.6 0.7 pad_convert_fusion
  1.3 0.2 multiply_cosine_fusion
  1.5 0.7 multiply_convert_fusion.embed
  2.2 2.2 %copy.12 = bf16[1,1280,320]{2,1,0:T(8,128)(2,1)} copy(bf16[1,1280,320]{1,2,0:T(8,128)(2,1)} %param.14) | data formatting | bytes 1638400 | tf_op args[6]
  4.4 165.9 %shard_map.111 = (f32[360,320]{1,0:T(8,128)}, f32[120,320]{1,0:T(8,128)}, f32[8,320]{1,0:T(8,128)}) custom-call(s32[2]{0:T(128)} %counts.1, bf16[2,2,2,24,320]{4,3,2,1,0:T(8,128)(2,1)} %latents.1, bf16[2,2,2,24,320]{4,3,2,1,0:T(8,128)(2,1)} %cotangent.1, bf16[16,1280]{1,0:T(8,128)(2,1)} %multiply_convert_fusion.embed, bf16[9,320,320]{2,1,0:T(8,128)(2,1)} %bitcast.8, ...), custom_call_target="tpu_custom_call" | custom-call | tf_op jit(solution)/shard_map/pallas_call | solution.py:469
  170.3 2.0 %copy.13 = f32[1,360,320]{1,2,0:T(8,128)} copy(f32[1,360,320]{2,1,0:T(8,128)} %bitcast.10) | data formatting | bytes 921600
  172.4 1.7 copy.14
  174.1 0.8 slice_reduce_fusion.1
  174.9 0.8 dynamic-slice_convert_fusion
  175.7 0.8 multiply_add_fusion
  176.5 0.6 constant_dynamic-slice_fusion
  (2 shorter events, 0.0 us)

commit v4 on v3

--- a/solution.py
+++ b/solution.py
@@ -28,15 +28,16 @@
 
 
 PAD = 32
-BLOCK = F_DEV * CLIPS * PAD
+BLOCK = F_DEV * PAD
 CELLS = R_DEV * BLOCK
-HALF = CLIPS * PAD
+LINKS = 12
+TURNS = 2 * CLIPS + 1
 MESH = pl.DeviceIdType.MESH
 
 
 def swap_order(flat):
     return jnp.concatenate(
-        [flat[:HALF], flat[2 * HALF : 3 * HALF], flat[HALF : 2 * HALF], flat[3 * HALF :]], axis=0
+        [flat[:PAD], flat[2 * PAD : 3 * PAD], flat[PAD : 2 * PAD], flat[3 * PAD :]], axis=0
     )
 
 
@@ -97,16 +98,17 @@
     column = lax.broadcasted_iota(jnp.int32, (R_DEV * F_DEV, PAD, 1), 1)
     for clip in range(CLIPS):
         live = (place < counts[clip]) & (column < WIDTH)
-        mask[:, clip] = jnp.where(live, 1.0, 0.0)
+        mask[clip] = jnp.where(live, 1.0, 0.0)
     column = lax.broadcasted_iota(jnp.int32, (CELLS // PAD, PAD, 1), 1)
     width_mask[...] = jnp.where(column < WIDTH, 1.0, 0.0).reshape(CELLS, 1)
     ids = [lax.broadcasted_iota(jnp.int32, (C, C), dim).astype(jnp.float32) for dim in range(2)]
     ids = [jnp.floor((one + 0.5) * (G / C)) for one in ids]
     groups[...] = jnp.where(ids[0] == ids[1], 1.0, 0.0)
     bias[...] = dot_nn(embed[...], time_kernel[...])
-    line = lax.broadcasted_iota(jnp.int32, (8, C), 0)
-    in_use = jnp.where(line < 2, counts[0], counts[1]).astype(jnp.float32)
-    inv_total = 1.0 / (in_use * (R_DEV * n_row * WIDTH * (C // G)))
+    inv_totals = []
+    for clip in range(CLIPS):
+        in_use = jnp.full((8, C), counts[clip], jnp.int32).astype(jnp.float32)
+        inv_totals.append(1.0 / (in_use * (R_DEV * n_row * WIDTH * (C // G))))
 
     barrier = pltpu.get_barrier_semaphore()
 
@@ -135,10 +137,17 @@
     after = (jnp.minimum(seg + 1, last), frame, row)
     before = (jnp.maximum(seg - 1, 0), frame, row)
     far = (last - seg, frame, row)
-    x_copy = remote(x_out, x_in, 0, after)
-    skip_copy = remote(x_out, skip_in, 1, far)
-    u_copy = remote(u_out, u_in, 10, before)
-    u_skip_copy = remote(u_out, u_skip, 11, far)
+
+    def hops(source, target, sem, device):
+        return [
+            remote(source.at[clip], target.at[clip], sem + LINKS * clip, device)
+            for clip in range(CLIPS)
+        ]
+
+    x_copy = hops(x_out, x_in, 0, after)
+    skip_copy = hops(x_out, skip_in, 1, far)
+    u_copy = hops(u_out, u_in, 10, before)
+    u_skip_copy = hops(u_out, u_skip, 11, far)
 
     def halo_start(padded, sem, index, size, at):
         onward = remote(
@@ -185,7 +194,7 @@
         for step in range(1, peers):
             copy = remote(
                 stat_src.at[turn], slots.at[turn, step - 1],
-                12 + turn * (peers - 1) + step - 1, member((me + step) % peers),
+                LINKS * CLIPS + turn * (peers - 1) + step - 1, member((me + step) % peers),
             )
             copy.start()
             pending.append((None, copy))
@@ -203,7 +212,7 @@
     def column_sum(values):
         return jnp.sum(values.reshape(-1, C), axis=0, keepdims=True)
 
-    def grouped(total):
+    def grouped(total, inv_total):
         return lax.dot_general(
             total * inv_total, groups[...], (((1,), (0,)), ((), ())),
             precision=lax.Precision.HIGHEST, preferred_element_type=jnp.float32,
@@ -211,7 +220,7 @@
 
     fused = bool(reduction)
     temporal_sum, spatial_sum = reduction[:2] if fused else (temporal_out, spatial_out)
-    first_sem = 12 + 3 * (peers - 1)
+    first_sem = LINKS * CLIPS + TURNS * (peers - 1)
 
     def stage(total, buffers):
         staged = buffers[0]
@@ -258,8 +267,7 @@
             total = total + arrived[step - 1].astype(jnp.float32)
         result[...] = total[: result.shape[0]]
 
-    def spatial_pass(padded, wide, sem, term):
-        halo = row_start(padded, sem)
+    def spatial_pass(padded, wide, halo, term):
         widen(padded, wide, BLOCK, CELLS)
         total = term(1, 0) + term(1, 1) + term(1, 2)
         halo_wait(halo)
@@ -270,177 +278,185 @@
                 total = total + term(a, b)
         return total
 
-    def temporal_pass(padded, sem, term):
-        halo = frame_start(padded, sem)
+    def temporal_pass(halo, term):
         total = term(1)
         halo_wait(halo)
         return total + term(0) + term(2)
 
+    def both(padded):
+        return jnp.concatenate([padded[clip, own, :] for clip in range(CLIPS)], axis=0)
+
     def turn():
-        for b in range(3):
-            x_turned[b] = jnp.transpose(wide_x[b], (1, 0))
-        a_turned[...] = jnp.transpose(pad_a[...], (1, 0))
+        for clip in range(CLIPS):
+            part = pl.ds(clip * CELLS, CELLS)
+            for a in range(3):
+                for b in range(3):
+                    rows = wide_x[clip, b, pl.ds(a * BLOCK, CELLS), :]
+                    x_turned[3 * a + b, :, part] = jnp.transpose(rows, (1, 0))
+                rows = pad_a[clip, pl.ds(a * BLOCK, CELLS), :]
+                a_turned[a, :, part] = jnp.transpose(rows, (1, 0))
 
     def temporal_grad():
+        upstream = both(pad_u)
         for k in range(3):
-            temporal_sum[pl.ds(k * C, C), :] = dot_nn(
-                a_turned[:, pl.ds(k * BLOCK, CELLS)], pad_u[own, :]
-            )
+            temporal_sum[pl.ds(k * C, C), :] = dot_nn(a_turned[k], upstream)
         if fused:
             stage(temporal_sum, reduction[2:6])
 
     own = pl.ds(BLOCK, CELLS)
-
-    @pl.when(seg == 0)
-    def _():
-        pad_x[own, :] = jnp.zeros((CELLS, C), jnp.bfloat16)
-        for r in range(R_DEV):
-            for f in range(F_DEV):
-                for clip in range(CLIPS):
-                    start = BLOCK + ((r * F_DEV + f) * CLIPS + clip) * PAD
-                    pad_x[pl.ds(start, WIDTH), :] = latents[clip, f, r]
-
-    @pl.when(seg > 0)
-    def _():
-        x_copy.wait_recv()
-
-    @pl.when((seg > 0) & (seg < last))
-    def _():
-        pad_x[own, :] = x_in[...]
-
-    @pl.when(seg == last)
-    def _():
-        skip_copy.wait_recv()
-        joined = x_in[...].astype(jnp.float32) + skip_in[...].astype(jnp.float32)
-        pad_x[own, :] = joined.astype(jnp.bfloat16)
-
-    hidden = spatial_pass(
-        pad_x, wide_x, 2,
-        lambda a, b: dot_nn(wide_x[b, pl.ds(a * BLOCK, CELLS), :], kernel[3 * a + b]),
-    )
-    normed[...] = hidden.reshape(normed.shape)
-    rows = []
-    for clip in range(CLIPS):
-        part = normed[:, clip] + bias[pl.ds(clip, 1), :].reshape(1, 1, C)
-        normed[:, clip] = part
-        masked = part * mask[:, clip]
-        rows += [column_sum(masked), column_sum(masked * part)]
-    stats = exchange_start(0, rows)
-    stats = grouped(exchange_wait(stats))
+    stats = []
+    for clip in range(CLIPS):
+
+        @pl.when(seg == 0)
+        def _():
+            pad_x[clip, own, :] = jnp.zeros((CELLS, C), jnp.bfloat16)
+            for r in range(R_DEV):
+                for f in range(F_DEV):
+                    start = BLOCK + (r * F_DEV + f) * PAD
+                    pad_x[clip, pl.ds(start, WIDTH), :] = latents[clip, f, r]
+
+        @pl.when(seg > 0)
+        def _():
+            x_copy[clip].wait_recv()
+
+        @pl.when((seg > 0) & (seg < last))
+        def _():
+            pad_x[clip, own, :] = x_in[clip]
+
+        @pl.when(seg == last)
+        def _():
+            skip_copy[clip].wait_recv()
+            joined = x_in[clip].astype(jnp.float32) + skip_in[clip].astype(jnp.float32)
+            pad_x[clip, own, :] = joined.astype(jnp.bfloat16)
+
+        wide = wide_x.at[clip]
+        hidden = spatial_pass(
+            pad_x.at[clip], wide, row_start(pad_x.at[clip], 2 + LINKS * clip),
+            lambda a, b: dot_nn(wide[b, pl.ds(a * BLOCK, CELLS), :], kernel[3 * a + b]),
+        )
+        hidden = hidden + bias[pl.ds(clip, 1), :]
+        part = hidden.reshape(R_DEV * F_DEV, PAD, C)
+        normed[clip] = part
+        masked = part * mask[clip]
+        stats.append(exchange_start(clip, [column_sum(masked), column_sum(masked * part)]))
     inverses = []
-    for clip in range(CLIPS):
-        mean = stats[2 * clip : 2 * clip + 1]
-        variance = stats[2 * clip + 1 : 2 * clip + 2] - mean * mean
-        inverse = lax.rsqrt(variance + EPSILON)
+    halos = []
+    for clip in range(CLIPS):
+        group = grouped(exchange_wait(stats[clip]), inv_totals[clip])
+        mean = group[0:1]
+        inverse = lax.rsqrt(group[1:2] - mean * mean + EPSILON)
         inverses.append(inverse)
-        part = (normed[:, clip] - mean.reshape(1, 1, C)) * inverse.reshape(1, 1, C)
-        normed[:, clip] = part
+        part = (normed[clip] - mean.reshape(1, 1, C)) * inverse.reshape(1, 1, C)
+        normed[clip] = part
         scaled = part * gain[...].reshape(1, 1, C)
-        grads[:, clip] = mask[:, clip] * (scaled * jax.nn.sigmoid(scaled))
-    pad_a[own, :] = swap_order(grads[...].reshape(CELLS, C)).astype(jnp.bfloat16)
-    temporal = temporal_pass(
-        pad_a, 4, lambda k: dot_nn(pad_a[pl.ds(k * BLOCK, CELLS), :], tkernel[k])
-    )
-
-    @pl.when(seg < last)
-    def _():
-        x_out[...] = (pad_x[own, :].astype(jnp.float32) + swap_order(temporal)).astype(jnp.bfloat16)
-
-    start_if(seg < last, x_copy)
-    start_if(seg == 0, skip_copy)
+        active = mask[clip] * (scaled * jax.nn.sigmoid(scaled))
+        pad_a[clip, own, :] = swap_order(active.reshape(CELLS, C)).astype(jnp.bfloat16)
+        halos.append(frame_start(pad_a.at[clip], 4 + LINKS * clip))
+    for clip in range(CLIPS):
+        temporal = temporal_pass(
+            halos[clip], lambda k: dot_nn(pad_a[clip, pl.ds(k * BLOCK, CELLS), :], tkernel[k])
+        )
+
+        @pl.when(seg < last)
+        def _():
+            total = pad_x[clip, own, :].astype(jnp.float32) + swap_order(temporal)
+            x_out[clip] = total.astype(jnp.bfloat16)
+
+        start_if(seg < last, x_copy[clip])
+        start_if(seg == 0, skip_copy[clip])
     pl.when(seg < last)(turn)
 
-    @pl.when(seg == last)
-    def _():
-        pad_u[own, :] = jnp.zeros((CELLS, C), jnp.bfloat16)
-        for r in range(R_DEV):
-            for f in range(F_DEV):
-                for clip in range(CLIPS):
-                    start = BLOCK + ((f * R_DEV + r) * CLIPS + clip) * PAD
-                    kept = mask[r * F_DEV + f, clip][:WIDTH]
+    gain_part = jnp.zeros((1, C), jnp.float32)
+    moments = []
+    for clip in range(CLIPS):
+
+        @pl.when(seg == last)
+        def _():
+            pad_u[clip, own, :] = jnp.zeros((CELLS, C), jnp.bfloat16)
+            for r in range(R_DEV):
+                for f in range(F_DEV):
+                    start = BLOCK + (f * R_DEV + r) * PAD
+                    kept = mask[clip, r * F_DEV + f][:WIDTH]
                     value = kept * cotangent[clip, f, r].astype(jnp.float32)
-                    pad_u[pl.ds(start, WIDTH), :] = value.astype(jnp.bfloat16)
-
-    @pl.when(seg < last)
-    def _():
-        u_copy.wait_recv()
-
-    @pl.when((seg > 0) & (seg < last))
-    def _():
-        pad_u[own, :] = swap_order(u_in[...])
-
-    @pl.when(seg == 0)
-    def _():
-        u_skip_copy.wait_recv()
-        joined = u_in[...].astype(jnp.float32) + u_skip[...].astype(jnp.float32)
-        pad_u[own, :] = swap_order(joined.astype(jnp.bfloat16))
-
-    act_grad = temporal_pass(
-        pad_u, 6, lambda k: dot_nt(pad_u[pl.ds(k * BLOCK, CELLS), :], tkernel[2 - k])
-    )
-    grads[...] = swap_order(act_grad).reshape(grads.shape)
-    rows = []
-    gain_part = jnp.zeros((1, C), jnp.float32)
-    for clip in range(CLIPS):
-        part = normed[:, clip]
+                    pad_u[clip, pl.ds(start, WIDTH), :] = value.astype(jnp.bfloat16)
+
+        @pl.when(seg < last)
+        def _():
+            u_copy[clip].wait_recv()
+
+        @pl.when((seg > 0) & (seg < last))
+        def _():
+            pad_u[clip, own, :] = swap_order(u_in[clip])
+
+        @pl.when(seg == 0)
+        def _():
+            u_skip_copy[clip].wait_recv()
+            joined = u_in[clip].astype(jnp.float32) + u_skip[clip].astype(jnp.float32)
+            pad_u[clip, own, :] = swap_order(joined.astype(jnp.bfloat16))
+
+        act_grad = temporal_pass(
+            frame_start(pad_u.at[clip], 6 + LINKS * clip),
+            lambda k: dot_nt(pad_u[clip, pl.ds(k * BLOCK, CELLS), :], tkernel[2 - k]),
+        )
+        act_grad = swap_order(act_grad).reshape(R_DEV * F_DEV, PAD, C)
+        part = normed[clip]
         scaled = part * gain[...].reshape(1, 1, C)
         gate = jax.nn.sigmoid(scaled)
-        scaled_grad = grads[:, clip] * mask[:, clip] * gate * (1.0 + scaled * (1.0 - gate))
+        scaled_grad = act_grad * mask[clip] * gate * (1.0 + scaled * (1.0 - gate))
+        normed_grad = scaled_grad * gain[...].reshape(1, 1, C)
+        grads[clip] = normed_grad
+        rows = [column_sum(normed_grad), column_sum(normed_grad * part)]
+        moments.append(exchange_start(CLIPS + clip, rows))
         gain_part = gain_part + column_sum(scaled_grad * part)
-        normed_grad = scaled_grad * gain[...].reshape(1, 1, C)
-        grads[:, clip] = normed_grad
-        rows += [column_sum(normed_grad), column_sum(normed_grad * part)]
-    moments = exchange_start(1, rows)
     pl.when(seg == 0)(temporal_grad)
-    moments = grouped(exchange_wait(moments))
     rows = []
     for clip in range(CLIPS):
-        first = moments[2 * clip : 2 * clip + 1].reshape(1, 1, C)
-        second = moments[2 * clip + 1 : 2 * clip + 2].reshape(1, 1, C)
+        group = grouped(exchange_wait(moments[clip]), inv_totals[clip])
+        first, second = group[0:1].reshape(1, 1, C), group[1:2].reshape(1, 1, C)
         part = inverses[clip].reshape(1, 1, C) * (
-            grads[:, clip] - mask[:, clip] * (first + normed[:, clip] * second)
-        )
-        part = part.astype(jnp.bfloat16).astype(jnp.float32)
-        grads[:, clip] = part
-        rows.append(column_sum(part))
-    pad_h[own, :] = grads[...].reshape(CELLS, C).astype(jnp.bfloat16)
+            grads[clip] - mask[clip] * (first + normed[clip] * second)
+        )
+        part = part.astype(jnp.bfloat16)
+        pad_h[clip, own, :] = part.reshape(CELLS, C)
+        rows.append(column_sum(part.astype(jnp.float32)))
+
     @pl.when(seg > 0)
     def _():
         pending_before = len(pending)
-        back = spatial_pass(
-            pad_h, wide_h, 8,
-            lambda a, b: dot_nt(wide_h[b, pl.ds(a * BLOCK, CELLS), :], kernel[8 - 3 * a - b]),
-        )
-        upstream = swap_order(pad_u[own, :]).astype(jnp.float32)
-        u_out[...] = (upstream + back * width_mask[...]).astype(jnp.bfloat16)
-        u_copy.start()
+        halos = [row_start(pad_h.at[clip], 8 + LINKS * clip) for clip in range(CLIPS)]
+        for clip in range(CLIPS):
+            wide = wide_h.at[clip]
+            back = spatial_pass(
+                pad_h.at[clip], wide, halos[clip],
+                lambda a, b: dot_nt(wide[b, pl.ds(a * BLOCK, CELLS), :], kernel[8 - 3 * a - b]),
+            )
+            upstream = swap_order(pad_u[clip, own, :]).astype(jnp.float32)
+            u_out[clip] = (upstream + back * width_mask[...]).astype(jnp.bfloat16)
+            u_copy[clip].start()
+            pl.when(seg == last)(u_skip_copy[clip].start)
         for condition, copy in pending[pending_before:]:
             pl.when(condition)(copy.wait_send)
         del pending[pending_before:]
 
-    @pl.when(seg == last)
-    def _():
-        u_skip_copy.start()
-        turn()
-
+    pl.when(seg == last)(turn)
     pl.when(seg > 0)(temporal_grad)
-    sums = exchange_start(2, rows + [gain_part])
+    sums = exchange_start(2 * CLIPS, rows + [gain_part])
     if fused:
         temporal_pair = pair_start(reduction[2:6], 0)
+    hidden_grad = both(pad_h)
     for a in range(3):
         if fused and a == 1:
             temporal_line = line_start(reduction[2:6], 0, temporal_pair)
         for b in range(3):
-            spatial_sum[pl.ds((3 * a + b) * C, C), :] = dot_nn(
-                x_turned[b, :, pl.ds(a * BLOCK, CELLS)], pad_h[own, :]
-            )
+            spatial_sum[pl.ds((3 * a + b) * C, C), :] = dot_nn(x_turned[3 * a + b], hidden_grad)
     if fused:
         stage(spatial_sum, reduction[6:10])
         spatial_line = line_start(reduction[6:10], 1, pair_start(reduction[6:10], 1))
         line_finish(reduction[2:6], temporal_line, temporal_out)
         line_finish(reduction[6:10], spatial_line, spatial_out)
     sums_out[...] = exchange_wait(sums)
-    for condition, copy in pending + [(seg > 0, u_copy), (seg == last, u_skip_copy)]:
+    pending += [(seg > 0, copy) for copy in u_copy] + [(seg == last, copy) for copy in u_skip_copy]
+    for condition, copy in pending:
         if condition is None:
             copy.wait_send()
         else:
@@ -450,10 +466,10 @@
 def run_section(sections, n_frame, n_row, *operands):
     peers = n_frame * n_row
     fused = n_frame == 2 and C * 3 % (8 * peers) == 0
-    flat = pltpu.VMEM((CELLS, C), jnp.bfloat16)
-    padded = pltpu.VMEM((2 * CELLS, C), jnp.bfloat16)
-    field = pltpu.VMEM((R_DEV * F_DEV, CLIPS, PAD, C), jnp.float32)
-    sems = 12 + 3 * (peers - 1) + 2 * n_row
+    flat = pltpu.VMEM((CLIPS, CELLS, C), jnp.bfloat16)
+    padded = pltpu.VMEM((CLIPS, 2 * CELLS, C), jnp.bfloat16)
+    field = pltpu.VMEM((CLIPS, R_DEV * F_DEV, PAD, C), jnp.float32)
+    sems = LINKS * CLIPS + TURNS * (peers - 1) + 2 * n_row
     vmem = pl.BlockSpec(memory_space=pltpu.VMEM)
     smem = pl.BlockSpec(memory_space=pltpu.SMEM)
     taps = (3, 9)
@@ -477,15 +493,15 @@
         out_specs=(vmem, vmem, vmem),
         scratch_shapes=[flat] * 6
         + [padded] * 4
-        + [pltpu.VMEM((3, 2 * CELLS, C), jnp.bfloat16)] * 2
+        + [pltpu.VMEM((CLIPS, 3, 2 * CELLS, C), jnp.bfloat16)] * 2
         + [
-            pltpu.VMEM((3, C, 2 * CELLS), jnp.bfloat16),
-            pltpu.VMEM((C, 2 * CELLS), jnp.bfloat16),
+            pltpu.VMEM((9, C, CLIPS * CELLS), jnp.bfloat16),
+            pltpu.VMEM((3, C, CLIPS * CELLS), jnp.bfloat16),
             field,
             field,
-            pltpu.VMEM((3, 8, C), jnp.float32),
-            pltpu.VMEM((3, peers - 1, 8, C), jnp.float32),
-            pltpu.VMEM((R_DEV * F_DEV, CLIPS, PAD, 1), jnp.float32),
+            pltpu.VMEM((TURNS, 8, C), jnp.float32),
+            pltpu.VMEM((TURNS, peers - 1, 8, C), jnp.float32),
+            pltpu.VMEM((CLIPS, R_DEV * F_DEV, PAD, 1), jnp.float32),
             pltpu.VMEM((CELLS, 1), jnp.float32),
             pltpu.VMEM((C, C), jnp.float32),
             pltpu.VMEM((16, C), jnp.float32),

time: 177 us -> 188 us (1.062)
  Pallas kernels: 166 us -> 177 us
    pallas_call x1, Pallas kernels: 166 us -> 177 us  [run_section(): pl.pallas_call(functools.partial(section_kernel, sections, n_frame, n_row...]
where the time goes in v4:
time: 188 us
  Pallas kernels  177 us (94%)
  local copies, waits for them, and re-layouts  7.39 us (4%)
  other arithmetic  3.14 us (2%)
    pallas_call x1, Pallas kernels, run_section(): pl.pallas_call(functools.partial(section_kernel, sections, n_frame, n_row...  177 us
    unnamed x3, local copies, waits for them, and re-layouts  5.97 us

profile of v4, /device:TPU:0, one launch (start us, length us, event | category | flops | bytes accessed | tf_op | source)
XLA Modules:
  0.0 187.8 jit_solution(7378871186790698188)
XLA Ops:
  0.6 0.7 pad_convert_fusion
  1.3 0.2 multiply_cosine_fusion
  1.5 0.7 multiply_convert_fusion.embed
  2.2 2.2 %copy.12 = bf16[1,1280,320]{2,1,0:T(8,128)(2,1)} copy(bf16[1,1280,320]{1,2,0:T(8,128)(2,1)} %param.14) | data formatting | bytes 1638400 | tf_op args[6]
  4.4 176.6 %shard_map.111 = (f32[360,320]{1,0:T(8,128)}, f32[120,320]{1,0:T(8,128)}, f32[8,320]{1,0:T(8,128)}) custom-call(s32[2]{0:T(128)} %counts.1, bf16[2,2,2,24,320]{4,3,2,1,0:T(8,128)(2,1)} %latents.1, bf16[2,2,2,24,320]{4,3,2,1,0:T(8,128)(2,1)} %cotangent.1, bf16[16,1280]{1,0:T(8,128)(2,1)} %multiply_convert_fusion.embed, bf16[9,320,320]{2,1,0:T(8,128)(2,1)} %bitcast.8, ...), custom_call_target="tpu_custom_call" | custom-call | tf_op jit(solution)/shard_map/pallas_call | solution.py:485
  181.0 2.0 %copy.13 = f32[1,360,320]{1,2,0:T(8,128)} copy(f32[1,360,320]{2,1,0:T(8,128)} %bitcast.10) | data formatting | bytes 921600
  183.0 1.7 copy.14
  184.7 0.8 slice_reduce_fusion.1
  185.6 0.8 dynamic-slice_convert_fusion
  186.4 0.8 multiply_add_fusion
  187.2 0.6 constant_dynamic-slice_fusion
  (2 shorter events, 0.0 us)

commit v5 on v3

--- a/solution.py
+++ b/solution.py
@@ -44,17 +44,13 @@
     return lax.dot_general(left, right, (((1,), (0,)), ((), ())), preferred_element_type=jnp.float32)
 
 
-def dot_nt(left, right):
-    return lax.dot_general(left, right, (((1,), (1,)), ((), ())), preferred_element_type=jnp.float32)
-
-
 def widen(padded, wide, start, length):
     some = pl.ds(start, length)
     values = padded[some, :]
     exact = values.astype(jnp.float32)
-    wide[0, some, :] = pltpu.roll(exact, 1, 0).astype(jnp.bfloat16)
-    wide[1, some, :] = values
-    wide[2, some, :] = pltpu.roll(exact, length - 1, 0).astype(jnp.bfloat16)
+    wide[some, :C] = pltpu.roll(exact, 1, 0).astype(jnp.bfloat16)
+    wide[some, C : 2 * C] = values
+    wide[some, 2 * C :] = pltpu.roll(exact, length - 1, 0).astype(jnp.bfloat16)
 
 
 def section_kernel(
@@ -62,7 +58,7 @@
     counts, latents, cotangent, embed, kernel, tkernel, time_kernel, gain,
     spatial_out, temporal_out, sums_out,
     x_in, skip_in, x_out, u_in, u_skip, u_out, pad_x, pad_a, pad_u, pad_h, wide_x, wide_h,
-    x_turned, a_turned, normed, grads, stat_src, slots, mask, width_mask, groups, bias,
+    x_turned, a_turned, normed, grads, stat_src, slots, mask, width_mask, groups, bias, kernel_back, tkernel_back,
     send_sem, recv_sem, *reduction,
 ):
     seg = lax.axis_index("segment")
@@ -261,14 +257,11 @@
     def spatial_pass(padded, wide, sem, term):
         halo = row_start(padded, sem)
         widen(padded, wide, BLOCK, CELLS)
-        total = term(1, 0) + term(1, 1) + term(1, 2)
+        total = term(1)
         halo_wait(halo)
         widen(padded, wide, 0, BLOCK)
         widen(padded, wide, 3 * BLOCK, BLOCK)
-        for a in (0, 2):
-            for b in range(3):
-                total = total + term(a, b)
-        return total
+        return total + term(0) + term(2)
 
     def temporal_pass(padded, sem, term):
         halo = frame_start(padded, sem)
@@ -277,9 +270,16 @@
         return total + term(0) + term(2)
 
     def turn():
-        for b in range(3):
-            x_turned[b] = jnp.transpose(wide_x[b], (1, 0))
+        x_turned[...] = jnp.transpose(wide_x[...], (1, 0))
         a_turned[...] = jnp.transpose(pad_a[...], (1, 0))
+
+    def turn_weights():
+        for k in range(3):
+            tkernel_back[k] = jnp.transpose(tkernel[2 - k], (1, 0))
+        for a in range(3):
+            for b in range(3):
+                tap = kernel[2 - a, pl.ds((2 - b) * C, C), :]
+                kernel_back[a, pl.ds(b * C, C), :] = jnp.transpose(tap, (1, 0))
 
     def temporal_grad():
         for k in range(3):
@@ -290,6 +290,7 @@
             stage(temporal_sum, reduction[2:6])
 
     own = pl.ds(BLOCK, CELLS)
+    pl.when(seg > 0)(turn_weights)
 
     @pl.when(seg == 0)
     def _():
@@ -316,7 +317,7 @@
 
     hidden = spatial_pass(
         pad_x, wide_x, 2,
-        lambda a, b: dot_nn(wide_x[b, pl.ds(a * BLOCK, CELLS), :], kernel[3 * a + b]),
+        lambda a: dot_nn(wide_x[pl.ds(a * BLOCK, CELLS), :], kernel[a]),
     )
     normed[...] = hidden.reshape(normed.shape)
     rows = []
@@ -349,6 +350,7 @@
     start_if(seg < last, x_copy)
     start_if(seg == 0, skip_copy)
     pl.when(seg < last)(turn)
+    pl.when(seg == 0)(turn_weights)
 
     @pl.when(seg == last)
     def _():
@@ -376,7 +378,7 @@
         pad_u[own, :] = swap_order(joined.astype(jnp.bfloat16))
 
     act_grad = temporal_pass(
-        pad_u, 6, lambda k: dot_nt(pad_u[pl.ds(k * BLOCK, CELLS), :], tkernel[2 - k])
+        pad_u, 6, lambda k: dot_nn(pad_u[pl.ds(k * BLOCK, CELLS), :], tkernel_back[k])
     )
     grads[...] = swap_order(act_grad).reshape(grads.shape)
     rows = []
@@ -409,7 +411,7 @@
         pending_before = len(pending)
         back = spatial_pass(
             pad_h, wide_h, 8,
-            lambda a, b: dot_nt(wide_h[b, pl.ds(a * BLOCK, CELLS), :], kernel[8 - 3 * a - b]),
+            lambda a: dot_nn(wide_h[pl.ds(a * BLOCK, CELLS), :], kernel_back[a]),
         )
         upstream = swap_order(pad_u[own, :]).astype(jnp.float32)
         u_out[...] = (upstream + back * width_mask[...]).astype(jnp.bfloat16)
@@ -430,10 +432,9 @@
     for a in range(3):
         if fused and a == 1:
             temporal_line = line_start(reduction[2:6], 0, temporal_pair)
-        for b in range(3):
-            spatial_sum[pl.ds((3 * a + b) * C, C), :] = dot_nn(
-                x_turned[b, :, pl.ds(a * BLOCK, CELLS)], pad_h[own, :]
-            )
+        spatial_sum[pl.ds(3 * a * C, 3 * C), :] = dot_nn(
+            x_turned[:, pl.ds(a * BLOCK, CELLS)], pad_h[own, :]
+        )
     if fused:
         stage(spatial_sum, reduction[6:10])
         spatial_line = line_start(reduction[6:10], 1, pair_start(reduction[6:10], 1))
@@ -477,9 +478,9 @@
         out_specs=(vmem, vmem, vmem),
         scratch_shapes=[flat] * 6
         + [padded] * 4
-        + [pltpu.VMEM((3, 2 * CELLS, C), jnp.bfloat16)] * 2
+        + [pltpu.VMEM((2 * CELLS, 3 * C), jnp.bfloat16)] * 2
         + [
-            pltpu.VMEM((3, C, 2 * CELLS), jnp.bfloat16),
+            pltpu.VMEM((3 * C, 2 * CELLS), jnp.bfloat16),
             pltpu.VMEM((C, 2 * CELLS), jnp.bfloat16),
             field,
             field,
@@ -489,6 +490,8 @@
             pltpu.VMEM((CELLS, 1), jnp.float32),
             pltpu.VMEM((C, C), jnp.float32),
             pltpu.VMEM((16, C), jnp.float32),
+            pltpu.VMEM((3, 3 * C, C), jnp.bfloat16),
+            pltpu.VMEM((3, C, C), jnp.bfloat16),
             pltpu.SemaphoreType.DMA((sems,)),
             pltpu.SemaphoreType.DMA((sems,)),
         ]
@@ -523,7 +526,7 @@
         latents,
         cotangent,
         time_embed,
-        spatial_weight[0],
+        spatial_weight[0].reshape(3, 3 * C, C),
         temporal_weight[0],
         time_weight[0],
         norm_gain,

time: 177 us -> 178 us (level)
  no operation moved by 1% of the time
where the time goes in v5:
time: 178 us
  Pallas kernels  167 us (94%)
  local copies, waits for them, and re-layouts  7.39 us (4%)
  other arithmetic  3.14 us (2%)
    pallas_call x1, Pallas kernels, run_section(): pl.pallas_call(functools.partial(section_kernel, sections, n_frame, n_row...  167 us
    unnamed x3, local copies, waits for them, and re-layouts  5.97 us

profile of v5, /device:TPU:0, one launch (start us, length us, event | category | flops | bytes accessed | tf_op | source)
XLA Modules:
  0.0 177.7 jit_solution(2563380262875418566)
XLA Ops:
  0.6 0.7 pad_convert_fusion
  1.3 0.2 multiply_cosine_fusion
  1.5 0.7 multiply_convert_fusion.embed
  2.2 2.2 %copy.12 = bf16[1,1280,320]{2,1,0:T(8,128)(2,1)} copy(bf16[1,1280,320]{1,2,0:T(8,128)(2,1)} %param.14) | data formatting | bytes 1638400 | tf_op args[6]
  4.4 166.5 %shard_map.111 = (f32[360,320]{1,0:T(8,128)}, f32[120,320]{1,0:T(8,128)}, f32[8,320]{1,0:T(8,128)}) custom-call(s32[2]{0:T(128)} %counts.1, bf16[2,2,2,24,320]{4,3,2,1,0:T(8,128)(2,1)} %latents.1, bf16[2,2,2,24,320]{4,3,2,1,0:T(8,128)(2,1)} %cotangent.1, bf16[16,1280]{1,0:T(8,128)(2,1)} %multiply_convert_fusion.embed, bf16[3,960,320]{2,1,0:T(8,128)(2,1)} %bitcast.8, ...), custom_call_target="tpu_custom_call" | custom-call | tf_op jit(solution)/shard_map/pallas_call | solution.py:470
  170.9 2.0 %copy.13 = f32[1,360,320]{1,2,0:T(8,128)} copy(f32[1,360,320]{2,1,0:T(8,128)} %bitcast.10) | data formatting | bytes 921600
  173.0 1.7 copy.14
  174.7 0.8 slice_reduce_fusion.1
  175.5 0.8 dynamic-slice_convert_fusion
  176.3 0.8 multiply_add_fusion
  177.1 0.6 constant_dynamic-slice_fusion
  (2 shorter events, 0.0 us)
